TPU v7x, 32 devices: a whole 2x2x4 slice. The times are simulated.
32 devices in a mesh: expert: 4 (over y, x), dp: 8 (over z, core).
Axes of the slice: x: 2, y: 2, z: 4, core: 2. Of those that a mesh axis runs over, the one named last changes fastest.
Arguments:
- tokens: bfloat16 [1024, 7168], P('dp', 'expert'), may hold values from -6 to 6
- grad_out: bfloat16 [1024, 7168], P('dp', 'expert'), may hold values from -6 to 6
- expert_ids: int32 [1024, 2], P('dp'), may hold values from -1 to 3, as said below
- route_weights: float32 [1024, 2], P('dp'), may hold values from 0.1 to 1
- w_gate: bfloat16 [4, 7168, 2048], P('expert', 'dp'), may hold values from -0.0625 to 0.0625
- w_up: bfloat16 [4, 7168, 2048], P('expert', 'dp'), may hold values from -0.0625 to 0.0625
- w_down: bfloat16 [4, 2048, 7168], P('expert', None, 'dp'), may hold values from -0.125 to 0.125
Outputs:
- grad_tokens: bfloat16 [1024, 7168], P('dp', 'expert')
- grad_gate: bfloat16 [4, 7168, 2048], P('expert', 'dp')
- grad_up: bfloat16 [4, 7168, 2048], P('expert', 'dp')
- grad_down: bfloat16 [4, 2048, 7168], P('expert', None, 'dp')
Inputs may be any that keep to these rules, and one draw needn't show every extreme that they name: expert_ids[t, 0] is an expert; expert_ids[t, 1] is another expert or -1. Within each block of 128 rows (the tokens of one index of dp) no expert appears in more than 64 rows, and one expert, the same in every block, appears in exactly 64 rows, each of which has -1 as its second entry.
All inputs are finite; a program needn't handle non-finite values.
Results may differ from a plain program's by a relative error of at most 0.03.
Values may be sent and summed in bfloat16 or wider, within the bound.
No kernel may reach another device: no remote copies, remote signals or barrier semaphores. Data moves between devices by JAX's collectives and lax.ppermute only.
A program may use at most 128 MiB of HBM per device.

v0:
```python
import functools
import math

import jax
import jax.numpy as jnp
from jax import lax
from jax.experimental import pallas as pl
from jax.experimental.pallas import tpu as pltpu
from jax.sharding import PartitionSpec as P

F32 = jnp.float32
BF16 = jnp.bfloat16
LAST_DIMS = (((1,), (1,)), ((), ()))
ROWS_FIRST = (((0,), (0,)), ((), ()))
FIXED = 5
PARTS = 2
PARAMS = pltpu.CompilerParams(vmem_limit_bytes=28 * 1024 * 1024)


def dot(a, b, dims=None):
    if dims is None:
        return jnp.dot(a, b, preferred_element_type=F32)
    return lax.dot_general(a, b, dims, preferred_element_type=F32)


def cost():
    return pl.CostEstimate(flops=1024, bytes_accessed=1024, transcendentals=0)


def in_hbm(*arrays):
    return [pltpu.with_memory_space_constraint(a, pltpu.HBM) for a in arrays]


def pass_on(scalar_ref, out_ref):
    for n in range(out_ref.shape[0]):
        out_ref[n] = scalar_ref[n]


def slot_one_hot(ids_ref, experts, capacity):
    tokens = ids_ref.shape[1]
    first, second = ids_ref[0:1, :], ids_ref[1:2, :]
    expert = lax.broadcasted_iota(jnp.int32, (8 * (-(-experts // 8)), tokens), 0)
    chosen = (first == expert) | (second == expert)
    before = lax.broadcasted_iota(jnp.int32, (tokens, tokens), 0) < lax.broadcasted_iota(
        jnp.int32, (tokens, tokens), 1
    )
    place = dot(chosen.astype(F32).astype(BF16), before.astype(F32).astype(BF16))
    place = jnp.where(chosen, place, -1.0).astype(jnp.int32)
    slot = lax.broadcasted_iota(jnp.int32, (capacity, tokens), 0)
    return [slot == place[e : e + 1, :] for e in range(experts)]


def dispatch_kernel(experts, weighted, scalar_ref, ids_hbm, weights_hbm, rows_hbm, *refs):
    *messages, hot_ref, token_ref, ids_ref, weights_ref, rows_ref, scale_ref, sems = refs
    _, capacity, feats = messages[0].shape
    pass_on(scalar_ref, token_ref)
    pairs = [(ids_hbm, ids_ref), (weights_hbm, weights_ref)]
    for h in range(2):
        whole = len(rows_hbm.shape) == 3
        half = rows_hbm.at[h] if whole else rows_hbm.at[:, pl.ds(h * feats, feats)]
        pairs.append((half, rows_ref.at[h]))
    copies = [pltpu.make_async_copy(a, b, sems.at[n]) for n, (a, b) in enumerate(pairs)]
    for copy in copies:
        copy.start()
    copies[0].wait()
    copies[1].wait()
    for e, hit in enumerate(slot_one_hot(ids_ref, experts, capacity)):
        place = slice(e * capacity, (e + 1) * capacity)
        hot_ref[place, :] = hit.astype(F32).astype(BF16)
        if weighted:
            weight = jnp.where(ids_ref[0:1, :] == e, weights_ref[0:1, :], weights_ref[1:2, :])
            weight = jnp.sum(jnp.where(hit, weight, 0.0), axis=1, keepdims=True)
            scale_ref[place, :] = jnp.broadcast_to(weight, (capacity, scale_ref.shape[1]))
    places = [
        pl.ds(pl.multiple_of((scalar_ref[4] ^ t) * capacity, capacity), capacity)
        for t in range(experts)
    ]
    hot = jnp.concatenate([hot_ref[place, :] for place in places], axis=0)
    for h in range(2):
        copies[2 + h].wait()
        out = dot(hot, rows_ref[h])
        for t, place in enumerate(places):
            part = out[t * capacity : (t + 1) * capacity]
            if weighted:
                part = part * scale_ref[place, 0:1]
            messages[t][h] = part.astype(BF16)


def dispatch_rows(scalars, ids, weights, rows, experts, weighted):
    tokens, feats = rows.shape[0], rows.shape[1] // 2
    capacity = tokens // 2
    if feats % 128:
        rows = rows.reshape(tokens, 2, feats).transpose(1, 0, 2)
    *messages, hot, token = pl.pallas_call(
        functools.partial(dispatch_kernel, experts, weighted),
        out_shape=[jax.ShapeDtypeStruct((2, capacity, feats), BF16)] * experts
        + [
            jax.ShapeDtypeStruct((experts * capacity, tokens), BF16),
            jax.ShapeDtypeStruct(scalars.shape, jnp.int32),
        ],
        in_specs=[pl.BlockSpec(memory_space=pltpu.SMEM)]
        + [pl.BlockSpec(memory_space=pltpu.HBM)] * 3,
        out_specs=[pl.BlockSpec(memory_space=pltpu.VMEM)] * (experts + 1)
        + [pl.BlockSpec(memory_space=pltpu.SMEM)],
        scratch_shapes=[
            pltpu.VMEM((2, tokens), jnp.int32),
            pltpu.VMEM((2, tokens), F32),
            pltpu.VMEM((2, tokens, feats), BF16),
            pltpu.VMEM((experts * capacity, 128), F32),
            pltpu.SemaphoreType.DMA((4,)),
        ],
        compiler_params=PARAMS,
        cost_estimate=cost(),
    )(scalars, *in_hbm(ids, weights, rows))
    return messages, hot, token


def assemble_kernel(scalar_ref, *refs):
    *messages, out_ref, sems = refs

    def copy(t, message):
        return pltpu.make_async_copy(message, out_ref.at[t ^ scalar_ref[4]], sems.at[t])

    for t, message in enumerate(messages):
        copy(t, message).start()
    for t, message in enumerate(messages):
        copy(t, message).wait()


def assemble(scalars, messages):
    return pl.pallas_call(
        assemble_kernel,
        out_shape=jax.ShapeDtypeStruct((len(messages), *messages[0].shape), BF16),
        in_specs=[pl.BlockSpec(memory_space=pltpu.SMEM)]
        + [pl.BlockSpec(memory_space=pl.ANY)] * len(messages),
        scratch_shapes=[pltpu.SemaphoreType.DMA((len(messages),))],
        compiler_params=PARAMS,
        cost_estimate=cost(),
    )(scalars, *messages)


def combine_kernel(experts, scalar_ref, hot_ref, *refs):
    pieces, (out_ref, rows_ref, sems) = refs[:-3], refs[-3:]
    capacity = pieces[0].shape[0]
    at = pl.program_id(0)

    def copy(n):
        return pltpu.make_async_copy(
            pieces[n], rows_ref.at[pl.ds(n * capacity, capacity)], sems.at[n]
        )

    @pl.when(at == 0)
    def _():
        for n in range(len(pieces)):
            copy(n).start()

    hot = jnp.concatenate(
        [
            hot_ref[pl.ds(pl.multiple_of((scalar_ref[2] ^ n) * capacity, capacity), capacity), :]
            for n in range(experts)
        ],
        axis=0,
    )
    for half in range(2):

        @pl.when(at == half)
        def _():
            for n in range(half * experts, (half + 1) * experts):
                copy(n).wait()
            rows = rows_ref[half * experts * capacity : (half + 1) * experts * capacity, :]
            out = dot(hot, rows, ROWS_FIRST).astype(BF16)
            out_ref[...] = out.reshape(out_ref.shape)


def combine_rows(scalars, hot, pieces, experts):
    tokens = hot.shape[1]
    capacity, feats = pieces[0].shape
    if feats % 128:
        out_shape = jax.ShapeDtypeStruct((2, tokens, feats), BF16)
        out_spec = pl.BlockSpec((1, tokens, feats), lambda a, c: (a ^ c[3], 0, 0))
    else:
        out_shape = jax.ShapeDtypeStruct((tokens, 2 * feats), BF16)
        out_spec = pl.BlockSpec((tokens, feats), lambda a, c: (0, a ^ c[3]))
    out = pl.pallas_call(
        functools.partial(combine_kernel, experts),
        out_shape=out_shape,
        grid_spec=pltpu.PrefetchScalarGridSpec(
            num_scalar_prefetch=1,
            grid=(2,),
            in_specs=[pl.BlockSpec((experts * capacity, tokens), lambda a, c: (0, 0))]
            + [pl.BlockSpec(memory_space=pltpu.HBM)] * len(pieces),
            out_specs=out_spec,
            scratch_shapes=[
                pltpu.VMEM((len(pieces) * capacity, feats), BF16),
                pltpu.SemaphoreType.DMA((len(pieces),)),
            ],
        ),
        compiler_params=PARAMS,
        cost_estimate=cost(),
    )(scalars, *in_hbm(hot, *pieces))
    if feats % 128:
        out = out.transpose(1, 0, 2).reshape(tokens, 2 * feats)
    return out


def gate_up_kernel(scalar_ref, x_ref, wg_ref, wu_ref, *outs):
    width = wg_ref.shape[1]

    @pl.when((pl.program_id(0) == 0) & (pl.program_id(1) == 0))
    def _():
        outs[2][...] = x_ref[...].T

    for own in range(2):

        @pl.when(pl.program_id(1) == own)
        def _():
            outs[own][0, :, :width] = dot(x_ref[...], wg_ref[...]).astype(BF16)
            outs[own][0, :, width:] = dot(x_ref[...], wu_ref[...]).astype(BF16)


def gate_up(scalars, x, w_gate, w_up, count):
    slots, feats = x.shape
    width = w_gate.shape[1] // (2 * count)
    out = jax.ShapeDtypeStruct((count, slots, 2 * width), BF16)
    out_spec = pl.BlockSpec((1, slots, 2 * width), lambda i, own, c: (i, 0, 0))
    column = pl.BlockSpec(
        (feats, width), lambda i, own, c: (0, c[FIXED + 2 * count + own * count + i])
    )
    return pl.pallas_call(
        gate_up_kernel,
        out_shape=(out, out, jax.ShapeDtypeStruct((feats, slots), BF16)),
        grid_spec=pltpu.PrefetchScalarGridSpec(
            num_scalar_prefetch=1,
            grid=(count, 2),
            in_specs=[pl.BlockSpec((slots, feats), lambda i, own, c: (0, 0)), column, column],
            out_specs=(
                out_spec,
                out_spec,
                pl.BlockSpec((feats, slots), lambda i, own, c: (0, 0)),
            ),
        ),
        compiler_params=PARAMS,
        cost_estimate=cost(),
    )(scalars, x, *in_hbm(w_gate, w_up))


def back_kernel(scalar_ref, g_ref, wd_ref, *refs):
    *shares, out_ref = refs
    back = dot(g_ref[...], wd_ref[...], LAST_DIMS)
    if not shares:
        out_ref[0] = back.astype(BF16)
        return
    sib_b, own_gu, sib_gu = shares
    width = back.shape[1]
    both = own_gu[0].astype(F32) + sib_gu[0].astype(F32)
    out_ref[0, :, : 2 * width] = both.astype(BF16)
    out_ref[0, :, 2 * width :] = (back + sib_b[0].astype(F32)).astype(BF16)


def back_rows(scalars, g, w_down, begin, size, count, shares):
    slots, feats = g.shape
    width = w_down.shape[0] // (2 * count)
    own = bool(shares)
    row = pl.BlockSpec(
        (width, feats), lambda i, c: (c[FIXED + 2 * count + own * count + begin + i], 0)
    )
    in_specs = [pl.BlockSpec((slots, feats), lambda i, c: (0, 0)), row]
    if own:
        in_specs.append(pl.BlockSpec((1, slots, width), lambda i, c: (i, 0, 0)))
        in_specs += [pl.BlockSpec((1, slots, 2 * width), lambda i, c: (begin + i, 0, 0))] * 2
    cols = (3 if own else 1) * width
    return pl.pallas_call(
        back_kernel,
        out_shape=jax.ShapeDtypeStruct((size, slots, cols), BF16),
        grid_spec=pltpu.PrefetchScalarGridSpec(
            num_scalar_prefetch=1,
            grid=(size,),
            in_specs=in_specs,
            out_specs=pl.BlockSpec((1, slots, cols), lambda i, c: (i, 0, 0)),
        ),
        compiler_params=PARAMS,
        cost_estimate=cost(),
    )(scalars, g, *in_hbm(w_down), *shares)


def activate(gate, upper, back):
    sig = jax.nn.sigmoid(gate)
    gated = gate * sig
    return (
        (gated * upper).astype(BF16),
        (back * upper * sig * (1.0 + gate * (1.0 - sig))).astype(BF16),
        (back * gated).astype(BF16),
    )


def hop_kernel(plan, scalar_ref, *refs):
    slot, count, chips, came = plan
    sums_ref = refs[-2]
    recv_ref = refs[0] if came else None
    send_ref = refs[-1]
    at = scalar_ref[0]
    width = send_ref.shape[1] // 3
    summing = (at <= slot) & (slot - at < count)

    def total(part):
        columns = slice(part * width, (part + 1) * width)
        value = sums_ref[0, :, columns].astype(F32)
        if came:
            value += jnp.where(at > 0, recv_ref[:, columns].astype(F32), 0.0)
        return value

    @pl.when(summing & (at < chips - 1))
    def _():
        for part in range(3):
            send_ref[:, part * width : (part + 1) * width] = total(part).astype(BF16)

    @pl.when(summing & (at == chips - 1))
    def _():
        for part, value in enumerate(activate(total(0), total(1), total(2))):
            send_ref[:, part * width : (part + 1) * width] = value

    if came:

        @pl.when(jnp.logical_not(summing))
        def _():
            send_ref[...] = recv_ref[...]


def hop(scalars, slot, count, chips, recv, sums, part):
    array, i = sums
    rows, cols = array.shape[1] // PARTS, array.shape[2]
    message = pl.BlockSpec((rows, cols), lambda n, c: (0, 0))
    operands, in_specs = [], []
    if recv is not None:
        operands.append(recv)
        in_specs.append(message)
    operands.append(array)
    in_specs.append(pl.BlockSpec((1, rows, cols), lambda n, c: (i, part, 0)))
    plan = (slot, count, chips, recv is not None)
    return pl.pallas_call(
        functools.partial(hop_kernel, plan),
        out_shape=jax.ShapeDtypeStruct((rows, cols), BF16),
        grid_spec=pltpu.PrefetchScalarGridSpec(
            num_scalar_prefetch=1,
            grid=(1,),
            in_specs=in_specs,
            out_specs=message,
        ),
        compiler_params=PARAMS,
        cost_estimate=cost(),
    )(scalars, *operands)


def choose_kernel(wanted, hops, scalar_ref, *refs):
    *candidates, sems = refs
    candidates, outs = candidates[:-wanted], candidates[-wanted:]
    rows = candidates[0].shape[0]

    def copy(k, n, part):
        return pltpu.make_async_copy(
            candidates[(k + n) * PARTS + part],
            outs[k].at[pl.ds(part * rows, rows)],
            sems.at[k, part],
        )

    for n in range(hops):

        @pl.when(scalar_ref[0] == n)
        def _():
            for k in range(wanted):
                for part in range(PARTS):
                    copy(k, n, part).start()

    for k in range(wanted):
        for part in range(PARTS):
            copy(k, 0, part).wait()


def choose(place, wanted, hops, candidates):
    rows, cols = candidates[0].shape
    return pl.pallas_call(
        functools.partial(choose_kernel, wanted, hops),
        out_shape=[jax.ShapeDtypeStruct((rows * PARTS, cols), BF16)] * wanted,
        in_specs=[pl.BlockSpec(memory_space=pltpu.SMEM)]
        + [pl.BlockSpec(memory_space=pl.ANY)] * len(candidates),
        scratch_shapes=[pltpu.SemaphoreType.DMA((wanted, PARTS))],
        compiler_params=PARAMS,
        cost_estimate=cost(),
    )(place, *candidates)


def forward_on_kernel(scalar_ref, in_ref, out_ref):
    out_ref[...] = in_ref[...]


def forward_on(scalars, message):
    return pl.pallas_call(
        forward_on_kernel,
        out_shape=jax.ShapeDtypeStruct(message.shape, message.dtype),
        in_specs=[
            pl.BlockSpec(memory_space=pltpu.SMEM),
            pl.BlockSpec(memory_space=pltpu.VMEM),
        ],
        compiler_params=PARAMS,
        cost_estimate=cost(),
    )(scalars, message)


def gradients_kernel(units, scale, first, scalar_ref, xt_ref, g_ref, *refs):
    messages, refs = refs[:units], refs[units if first else units + 3 :]
    gg_ref, gu_ref, gd_ref, token_ref = refs
    width = gg_ref.shape[1]
    pass_on(scalar_ref, token_ref)
    for u in range(units):

        @pl.when(pl.program_id(0) == u)
        def _():
            both = dot(xt_ref[...], messages[u][:, width:]) * scale
            gg_ref[...] = both[:, :width].astype(BF16)
            gu_ref[...] = both[:, width:].astype(BF16)
            scaled = messages[u][:, :width]
            gd_ref[...] = (dot(scaled, g_ref[...], ROWS_FIRST) * scale).astype(BF16)


def gradients(scalars, begin, count, scale, x_t, g, messages, grads):
    slots, feats = g.shape
    width = messages[0].shape[1] // 3
    hidden = 2 * count * width
    units = len(messages)

    def at(u, c):
        return c[FIXED + begin + u]

    column = pl.BlockSpec((feats, width), lambda u, c: (0, at(u, c)))
    in_specs = [
        pl.BlockSpec((feats, slots), lambda u, c: (0, 0)),
        pl.BlockSpec((slots, feats), lambda u, c: (0, 0)),
    ]
    in_specs += [pl.BlockSpec((slots, 3 * width), lambda u, c: (0, 0))] * units
    operands = [x_t, g, *messages]
    aliases = {}
    if grads is not None:
        aliases = {len(operands) + 1 + n: n for n in range(3)}
        operands += grads
        in_specs += [pl.BlockSpec(memory_space=pl.ANY)] * 3
    *grads, token = pl.pallas_call(
        functools.partial(gradients_kernel, units, scale, grads is None),
        out_shape=[
            jax.ShapeDtypeStruct((feats, hidden), BF16),
            jax.ShapeDtypeStruct((feats, hidden), BF16),
            jax.ShapeDtypeStruct((hidden, feats), BF16),
            jax.ShapeDtypeStruct(scalars.shape, jnp.int32),
        ],
        grid_spec=pltpu.PrefetchScalarGridSpec(
            num_scalar_prefetch=1,
            grid=(units,),
            in_specs=in_specs,
            out_specs=[
                column,
                column,
                pl.BlockSpec((width, feats), lambda u, c: (at(u, c), 0)),
                pl.BlockSpec(memory_space=pltpu.SMEM),
            ],
        ),
        input_output_aliases=aliases,
        compiler_params=PARAMS,
        cost_estimate=cost(),
    )(scalars, *operands)
    return grads, token


def sum_rows_kernel(units, pieces, scalar_ref, *refs):
    messages, weights, refs = refs[:units], refs[units : 3 * units], refs[3 * units :]
    width = weights[0].shape[1]
    both = jnp.concatenate([message[:, width:] for message in messages], axis=1)
    part = dot(both, jnp.concatenate([w[...] for w in weights], axis=1), LAST_DIMS)
    if not pieces:
        out_ref, token_ref = refs
        out_ref[...] = part
        pass_on(scalar_ref, token_ref)
        return
    acc_in, *outs, acc = refs
    acc[...] = acc_in[...] + part
    size = outs[0].shape[0]
    for n, out in enumerate(outs):
        start = pl.multiple_of((scalar_ref[1] ^ n) * size, size)
        out[...] = acc[pl.ds(start, size), :].astype(BF16)


def sum_rows(scalars, begin, messages, weights, acc, pieces):
    slots, width = messages[0].shape[0], messages[0].shape[1] // 3
    feats = weights[0].shape[0]
    units = len(messages)
    in_specs = [pl.BlockSpec((slots, 3 * width), lambda n, c: (0, 0))] * units
    operands = list(messages)
    for u in range(units):
        column = pl.BlockSpec((feats, width), lambda n, c, u=u: (0, c[FIXED + begin + u]))
        operands += in_hbm(*weights)
        in_specs += [column, column]
    whole = pl.BlockSpec((slots, feats), lambda n, c: (0, 0))
    if pieces:
        operands.append(acc)
        in_specs.append(whole)
        out_shape = [jax.ShapeDtypeStruct((slots // pieces, feats), BF16)] * pieces
        out_specs = [pl.BlockSpec((slots // pieces, feats), lambda n, c: (0, 0))] * pieces
        scratch = [pltpu.VMEM((slots, feats), F32)]
    else:
        out_shape = [
            jax.ShapeDtypeStruct((slots, feats), F32),
            jax.ShapeDtypeStruct(scalars.shape, jnp.int32),
        ]
        out_specs = [whole, pl.BlockSpec(memory_space=pltpu.SMEM)]
        scratch = []
    return pl.pallas_call(
        functools.partial(sum_rows_kernel, units, pieces),
        out_shape=out_shape,
        grid_spec=pltpu.PrefetchScalarGridSpec(
            num_scalar_prefetch=1,
            grid=(1,),
            in_specs=in_specs,
            out_specs=out_specs,
            scratch_shapes=scratch,
        ),
        compiler_params=PARAMS,
        cost_estimate=cost(),
    )(scalars, *operands)


def body(tokens, grad_out, expert_ids, route_weights, w_gate, w_up, w_down):
    experts = lax.axis_size("expert")
    groups = lax.axis_size("dp")
    tok_rows = tokens.shape[0]
    feats = w_gate.shape[1]
    capacity = tok_rows // 2
    chips = groups // 2
    count = chips
    assert groups == 2 * experts and tokens.shape[1] == 2 * feats
    inv_root = 1.0 / math.sqrt(tok_rows * groups)
    expert = lax.axis_index("expert").astype(jnp.int32)
    block = lax.axis_index("dp").astype(jnp.int32)
    chip, core = block // 2, block % 2
    along = jnp.where(core == 0, chip, chips - 1 - chip)
    w_gate, w_up, w_down = w_gate[0], w_up[0], w_down[0]
    ids, weights = expert_ids.T, route_weights.T

    swap = [(j, j ^ 1) for j in range(groups)]
    up = [2 * z for z in range(chips)]
    circle = up + [j + 1 for j in reversed(up)]
    ring = list(zip(circle, circle[1:] + circle[:1]))

    scalars = [along, expert + experts * core, block % experts, block // experts, expert]
    scalars += [(d ^ 1 ^ core) * count + k for d in range(2) for k in range(count)]
    scalars += [(1 - core) * count + (i - (chips - 1 - along)) % count for i in range(count)]
    scalars += [core * count + (i - along) % count for i in range(count)]
    scalars = jnp.stack(scalars).astype(jnp.int32)

    def exchange(messages):
        came = [messages[0]]
        for t in range(1, experts):
            came.append(lax.ppermute(messages[t], "expert", [(q, q ^ t) for q in range(experts)]))
        blocks = assemble(scalars, came).reshape(groups, capacity, feats)
        blocks = lax.all_to_all(blocks, "dp", split_axis=0, concat_axis=0, tiled=True)
        return blocks.reshape(groups * capacity, feats)

    x_messages, _, token = dispatch_rows(scalars, ids, weights, tokens, experts, False)
    g_messages, hot, _ = dispatch_rows(token, ids, weights, grad_out, experts, True)
    x = exchange(x_messages)
    g = exchange(g_messages)

    other_gu, own_gu, x_t = gate_up(scalars, x, w_gate, w_up, count)
    sib_gu = lax.ppermute(other_gu, "dp", swap)
    spans = ((0, count // 2), (count // 2, count - count // 2))
    others = [
        lax.ppermute(back_rows(scalars, g, w_down, begin, size, count, ()), "dp", swap)
        for begin, size in spans
    ]
    sums = []
    for (begin, size), sib_b in zip(spans, others):
        shares = (sib_b, own_gu, sib_gu)
        both = back_rows(scalars, g, w_down, begin, size, count, shares)
        sums += [(both, i) for i in range(size)]

    slots = 2 * count + chips - 2
    first_back = chips - 1 + count
    recv = []
    gate_and_up = (w_gate, w_up)
    place = along.astype(jnp.int32)[None]

    def pick(token, begin, wanted):
        found = recv[count - 1 + begin : count - 1 + begin + chips + wanted - 1]
        return choose(token, wanted, chips, [part for came in found for part in came])

    early = count - 1
    mine, grads = [], None
    for s in range(slots):
        came = []
        for part in range(PARTS):
            send = recv[s - 1][part] if s else None
            if s < first_back:
                send = hop(place, s, count, chips, send, sums[s % count], part)
            elif s > first_back and part == 0:
                k = len(mine)
                mine += pick(place, k, 1)
                grads, token = gradients(
                    scalars, k, count, inv_root, x_t, g, mine[-1:], grads
                )
                send = forward_on(token, send)
            came.append(lax.ppermute(send, "dp", ring))
        recv.append(came)

    ready = len(mine)
    mine += pick(place, ready, early - ready)
    others = [lax.ppermute(message, "dp", swap) for message in mine]
    acc, token = sum_rows(scalars, 0, mine, gate_and_up, None, 0)
    last = pick(token, early, count - early)
    grads, _ = gradients(
        token, ready, count, inv_root, x_t, g, mine[ready:], grads
    )
    mine = last
    others += [lax.ppermute(message, "dp", swap) for message in mine]
    units = [*mine, *others]
    pieces = sum_rows(scalars, early, units, gate_and_up, acc, groups)
    returned = []
    for r, piece in enumerate(pieces):
        pairs = []
        for q in range(experts):
            for b in range(groups):
                h, e = divmod(b ^ r, experts)
                pairs.append((e * groups + 2 * q + h, q * groups + b))
        returned.append(lax.ppermute(piece, ("expert", "dp"), pairs))
    grads, _ = gradients(scalars, early, count, inv_root, x_t, g, units, grads)
    grad_tokens = combine_rows(scalars, hot, returned, experts)
    return (grad_tokens, grads[0][None], grads[1][None], grads[2][None])


def solution(mesh):
    in_specs = (
        P("dp", "expert"),
        P("dp", "expert"),
        P("dp", None),
        P("dp", None),
        P("expert", "dp", None),
        P("expert", "dp", None),
        P("expert", None, "dp"),
    )
    out_specs = (
        P("dp", "expert"),
        P("expert", "dp", None),
        P("expert", "dp", None),
        P("expert", None, "dp"),
    )
    return jax.shard_map(body, mesh=mesh, in_specs=in_specs, out_specs=out_specs, check_vma=False)
```

profile of v0, /device:TPU:0, one launch (start us, length us, event | category | flops | bytes accessed | tf_op | source)
XLA Modules:
  0.0 216.0 jit_solution(2741130648044062091)
XLA Ops:
  3.4 3.0 %collective-permute-start.4 = (bf16[2,64,896]{2,1,0:T(8,128)(2,1)S(1)}, bf16[2,64,896]{2,1,0:T(8,128)(2,1)S(1)}, u32[]{:S(2)}, u32[]{:S(2)}) collective-permute-start(bf16[2,64,896]{2,1,0:T(8,128)(2,1)S(1)} %get-tuple-element.48), channel_id=1, source_target_pairs={{0,8},{8,0},{16,24},{24,16},{1,9},{9,1},{17,25},{25,17},{2,10},{10... | collective-permute-start | bytes 688136 | tf_op jit(solution)/shard_map/ppermute | solution.py:560
  8.0 4.9 %collective-permute-done.4.refs_1_ = bf16[2,64,896]{2,1,0:T(8,128)(2,1)S(1)} collective-permute-done((bf16[2,64,896]{2,1,0:T(8,128)(2,1)S(1)}, bf16[2,64,896]{2,1,0:T(8,128)(2,1)S(1)}, u32[]{:S(2)}, u32[]{:S(2)}) %collective-permute-start.4) | collective-permute-done | bytes 229408 | tf_op jit(solution)/shard_map/ppermute | solution.py:560
  12.9 5.5 %collective-permute-done.5.refs_2_ = bf16[2,64,896]{2,1,0:T(8,128)(2,1)S(1)} collective-permute-done((bf16[2,64,896]{2,1,0:T(8,128)(2,1)S(1)}, bf16[2,64,896]{2,1,0:T(8,128)(2,1)S(1)}, u32[]{:S(2)}, u32[]{:S(2)}) %collective-permute-start.5) | collective-permute-done | bytes 229408 | tf_op jit(solution)/shard_map/ppermute | solution.py:560
  18.4 2.7 %shard_map.106 = bf16[4,2,64,896]{3,2,1,0:T(8,128)(2,1)} custom-call(s32[21]{0:T(128)S(1)} %stack.87.scalar_ref, bf16[2,64,896]{2,1,0:T(8,128)(2,1)S(1)} %get-tuple-element.47.refs_0_, bf16[2,64,896]{2,1,0:T(8,128)(2,1)S(1)} %collective-permute-done.4.refs_1_, bf16[2,64,896]{2,1,0:T(8,128)(2,1)S(1)} %collective-permute-done.5.refs_2_, ...), custom_call_target="tpu_custom_call" | custom-call | flops 1024 | bytes 1024 | tf_op jit(solution)/shard_map/pallas_call | solution.py:131
  21.1 4.9 %all-to-all-start.1 = ((bf16[8,64,896]{2,1,0:T(8,128)(2,1)}), bf16[8,64,896]{2,1,0:T(8,128)(2,1)S(1)}, u32[]{:S(2)}, u32[]{:S(2)}) async-start(bf16[8,64,896]{2,1,0:T(8,128)(2,1)} %bitcast.26), calls=%async_computation.1 | async-start | bytes 1835008 | tf_op jit(solution)/shard_map/all_to_all | solution.py:562
  32.5 4.9 %collective-permute-done.refs_1_ = bf16[2,64,896]{2,1,0:T(8,128)(2,1)S(1)} collective-permute-done((bf16[2,64,896]{2,1,0:T(8,128)(2,1)S(1)}, bf16[2,64,896]{2,1,0:T(8,128)(2,1)S(1)}, u32[]{:S(2)}, u32[]{:S(2)}) %collective-permute-start) | collective-permute-done | bytes 229408 | tf_op jit(solution)/shard_map/ppermute | solution.py:560
  37.4 3.9 %collective-permute-done.1.refs_2_ = bf16[2,64,896]{2,1,0:T(8,128)(2,1)S(1)} collective-permute-done((bf16[2,64,896]{2,1,0:T(8,128)(2,1)S(1)}, bf16[2,64,896]{2,1,0:T(8,128)(2,1)S(1)}, u32[]{:S(2)}, u32[]{:S(2)}) %collective-permute-start.1) | collective-permute-done | bytes 229408 | tf_op jit(solution)/shard_map/ppermute | solution.py:560
  42.9 2.7 %shard_map.104 = bf16[4,2,64,896]{3,2,1,0:T(8,128)(2,1)} custom-call(s32[21]{0:T(128)S(1)} %stack.87.scalar_ref, bf16[2,64,896]{2,1,0:T(8,128)(2,1)S(1)} %get-tuple-element.43.refs_0_, bf16[2,64,896]{2,1,0:T(8,128)(2,1)S(1)} %collective-permute-done.refs_1_, bf16[2,64,896]{2,1,0:T(8,128)(2,1)S(1)} %collective-permute-done.1.refs_2_, ...), custom_call_target="tpu_custom_call" | custom-call | flops 1024 | bytes 1024 | tf_op jit(solution)/shard_map/pallas_call | solution.py:131
  45.6 4.2 %all-to-all-done.1 = bf16[8,64,896]{2,1,0:T(8,128)(2,1)S(1)} async-done(((bf16[8,64,896]{2,1,0:T(8,128)(2,1)}), bf16[8,64,896]{2,1,0:T(8,128)(2,1)S(1)}, u32[]{:S(2)}, u32[]{:S(2)}) %all-to-all-start.1) | async-done | bytes 917536 | tf_op jit(solution)/shard_map/all_to_all | solution.py:562
  49.8 3.6 %all-to-all-start = ((bf16[8,64,896]{2,1,0:T(8,128)(2,1)}), bf16[8,64,896]{2,1,0:T(8,128)(2,1)S(1)}, u32[]{:S(2)}, u32[]{:S(2)}) async-start(bf16[8,64,896]{2,1,0:T(8,128)(2,1)} %bitcast.23), calls=%async_computation | async-start | bytes 1835008 | tf_op jit(solution)/shard_map/all_to_all | solution.py:562
  53.4 10.7 %shard_map.107 = (bf16[4,512,512]{2,1,0:T(8,128)(2,1)}, bf16[4,512,512]{2,1,0:T(8,128)(2,1)S(1)}, bf16[896,512]{1,0:T(8,128)(2,1)S(1)}) custom-call(s32[21]{0:T(128)S(1)} %stack.87.scalar_ref, bf16[512,896]{1,0:T(8,128)(2,1)S(1)} %bitcast.41, bf16[896,2048]{1,0:T(8,128)(2,1)} %bitcast.42, bf16[896,2048]{1,0:T(8,128)(2,1)} %bitcast.51), custom_call_target="tpu_custom_call" | custom-call | flops 1024 | bytes 1024 | tf_op jit(solution)/shard_map/pallas_call | solution.py:229
  65.8 11.3 %all-to-all-done = bf16[8,64,896]{2,1,0:T(8,128)(2,1)S(1)} async-done(((bf16[8,64,896]{2,1,0:T(8,128)(2,1)}), bf16[8,64,896]{2,1,0:T(8,128)(2,1)S(1)}, u32[]{:S(2)}, u32[]{:S(2)}) %all-to-all-start) | async-done | bytes 917536 | tf_op jit(solution)/shard_map/all_to_all | solution.py:562
  77.1 2.6 %shard_map.105 = bf16[2,512,256]{2,1,0:T(8,128)(2,1)S(1)} custom-call(s32[21]{0:T(128)S(1)} %stack.87.scalar_ref, bf16[512,896]{1,0:T(8,128)(2,1)S(1)} %bitcast.33, bf16[2048,896]{1,0:T(8,128)(2,1)} %bitcast.60), custom_call_target="tpu_custom_call" | custom-call | flops 1024 | bytes 1024 | tf_op jit(solution)/shard_map/pallas_call | solution.py:272
  81.7 3.1 %shard_map.108.refs_0_.refs_1_ = bf16[2,512,768]{2,1,0:T(8,128)(2,1)S(1)} custom-call(s32[21]{0:T(128)S(1)} %stack.87.scalar_ref, bf16[512,896]{1,0:T(8,128)(2,1)S(1)} %bitcast.34, bf16[2048,896]{1,0:T(8,128)(2,1)} %bitcast.61, bf16[2,512,256]{2,1,0:T(8,128)(2,1)S(1)} %collective-permute-done.3.refs_0_, bf16[4,512,512]{2,1,0:T(8,128)(2,1)S(1)} %copy-done.1, ...), custom_call_target="tpu_custom_call" | custom-call | flops 1024 | bytes 1024 | tf_op jit(solution)/shard_map/pallas_call | solution.py:272
  97.0 3.1 %shard_map.112.refs_1_ = bf16[2,512,768]{2,1,0:T(8,128)(2,1)S(1)} custom-call(s32[21]{0:T(128)S(1)} %stack.87.scalar_ref, bf16[512,896]{1,0:T(8,128)(2,1)S(1)} %bitcast.36, bf16[2048,896]{1,0:T(8,128)(2,1)} %bitcast.63, bf16[2,512,256]{2,1,0:T(8,128)(2,1)S(1)} %collective-permute-done.10.refs_0_, bf16[4,512,512]{2,1,0:T(8,128)(2,1)S(1)} %copy-done.1, ...), custom_call_target="tpu_custom_call" | custom-call | flops 1024 | bytes 1024 | tf_op jit(solution)/shard_map/pallas_call | solution.py:272
  115.4 2.6 %collective-permute-start.17 = (bf16[256,768]{1,0:T(8,128)(2,1)S(1)}, bf16[256,768]{1,0:T(8,128)(2,1)S(1)}, u32[]{:S(2)}, u32[]{:S(2)}) collective-permute-start(bf16[256,768]{1,0:T(8,128)(2,1)S(1)} %shard_map.119), channel_id=1, source_target_pairs={{0,2},{2,4},{4,6},{6,7},{7,5},{5,3},{3,1},{1,0},{8,10},{10,12},{12... | collective-permute-start | bytes 1179656 | tf_op jit(solution)/shard_map/ppermute | solution.py:608
  119.6 2.6 %collective-permute-start.18 = (bf16[256,768]{1,0:T(8,128)(2,1)S(1)}, bf16[256,768]{1,0:T(8,128)(2,1)S(1)}, u32[]{:S(2)}, u32[]{:S(2)}) collective-permute-start(bf16[256,768]{1,0:T(8,128)(2,1)S(1)} %shard_map.120), channel_id=1, source_target_pairs={{0,2},{2,4},{4,6},{6,7},{7,5},{5,3},{3,1},{1,0},{8,10},{10,12},{12... | collective-permute-start | bytes 1179656 | tf_op jit(solution)/shard_map/ppermute | solution.py:608
  165.2 4.2 %shard_map.130 = (f32[512,896]{1,0:T(8,128)S(1)}, s32[21]{0:T(128)S(1)}) custom-call(s32[21]{0:T(128)S(1)} %stack.87.scalar_ref, bf16[512,768]{1,0:T(8,128)(2,1)S(1)} %shard_map.125.refs_0_, bf16[512,768]{1,0:T(8,128)(2,1)S(1)} %shard_map.126.refs_1_.refs_0_, bf16[512,768]{1,0:T(8,128)(2,1)S(1)} %shard_map.129.refs_2_.refs_0_, bf16[896,2048]{1,0:T(8,128)(2,1)} %bitcast.43, ...), custom_call_target="tpu_custom_call" | custom-call | flops 1024 | bytes 1024 | tf_op jit(solution)/shard_map/pallas_call | solution.py:514
  174.5 5.9 %shard_map.134 = (bf16[64,896]{1,0:T(8,128)(2,1)S(1)}, bf16[64,896]{1,0:T(8,128)(2,1)S(1)}, bf16[64,896]{1,0:T(8,128)(2,1)S(1)}, bf16[64,896]{1,0:T(8,128)(2,1)S...) custom-call(s32[21]{0:T(128)S(1)} %stack.87.scalar_ref, ...), custom_call_target="tpu_custom_call" | custom-call | flops 1024 | bytes 1024 | tf_op jit(solution)/shard_map/pallas_call | solution.py:514
  181.1 3.2 %collective-permute-start.34 = (bf16[64,896]{1,0:T(8,128)(2,1)S(1)}, bf16[64,896]{1,0:T(8,128)(2,1)S(1)}, u32[]{:S(2)}, u32[]{:S(2)}) collective-permute-start(bf16[64,896]{1,0:T(8,128)(2,1)S(1)} %get-tuple-element.62), channel_id=1, source_target_pairs={{8,0},{0,1},{24,2},{16,3},{9,4},{1,5},{25,6},{17,7},{10,8},{2,9},{... | collective-permute-start | bytes 344072 | tf_op jit(solution)/shard_map/ppermute | solution.py:630
  186.6 4.7 %collective-permute-start.36 = (bf16[64,896]{1,0:T(8,128)(2,1)S(1)}, bf16[64,896]{1,0:T(8,128)(2,1)S(1)}, u32[]{:S(2)}, u32[]{:S(2)}) collective-permute-start(bf16[64,896]{1,0:T(8,128)(2,1)S(1)} %get-tuple-element.64), channel_id=1, source_target_pairs={{24,0},{16,1},{8,2},{0,3},{25,4},{17,5},{9,6},{1,7},{26,8},{18,9},... | collective-permute-start | bytes 344072 | tf_op jit(solution)/shard_map/ppermute | solution.py:630
  193.2 4.6 %collective-permute-start.38 = (bf16[64,896]{1,0:T(8,128)(2,1)S(1)}, bf16[64,896]{1,0:T(8,128)(2,1)S(1)}, u32[]{:S(2)}, u32[]{:S(2)}) collective-permute-start(bf16[64,896]{1,0:T(8,128)(2,1)S(1)} %get-tuple-element.66), channel_id=1, source_target_pairs={{9,0},{1,1},{25,2},{17,3},{8,4},{0,5},{24,6},{16,7},{11,8},{3,9},{... | collective-permute-start | bytes 344072 | tf_op jit(solution)/shard_map/ppermute | solution.py:630
  204.6 6.6 %shard_map.137 = (bf16[896,2048]{1,0:T(8,128)(2,1)}, bf16[896,2048]{1,0:T(8,128)(2,1)}, bf16[2048,896]{1,0:T(8,128)(2,1)}, s32[21]{0:T(128)}) custom-call(s32[21]{0:T(128)S(1)} %stack.87.scalar_ref, bf16[896,512]{1,0:T(8,128)(2,1)S(1)} %get-tuple-element.53.xt_ref, ...), custom_call_target="tpu_custom_call", output_to_operand_aliasing={{0}: (8, {}), {1}: (9, {}), {2}: (10, {})} | custom-call | flops 1024 | bytes 1024 | tf_op jit(solution)/shard_map/pallas_call | solution.py:446
  212.0 3.8 %shard_map.135 = bf16[128,1792]{1,0:T(8,128)(2,1)} custom-call(s32[21]{0:T(128)S(1)} %stack.87.scalar_ref, bf16[256,128]{1,0:T(8,128)(2,1)} %copy-done.2, bf16[64,896]{1,0:T(8,128)(2,1)} %copy-done.3, bf16[64,896]{1,0:T(8,128)(2,1)} %copy-done.4, bf16[64,896]{1,0:T(8,128)(2,1)} %copy-done.5, bf16[64,896]{1,0:T(8,128)(2,1)} %copy-done.6, ...), custom_call_target="tpu_custom_call" | custom-call | flops 1024 | bytes 1024 | tf_op jit(solution)/shard_map/pallas_call | solution.py:184
  (121 shorter events, 105.2 us)
Async XLA Ops:
  3.4 9.4 %collective-permute-start.4 = (bf16[2,64,896]{2,1,0:T(8,128)(2,1)S(1)}, bf16[2,64,896]{2,1,0:T(8,128)(2,1)S(1)}, u32[]{:S(2)}, u32[]{:S(2)}) collective-permute-start(bf16[2,64,896]{2,1,0:T(8,128)(2,1)S(1)} %get-tuple-element.48), channel_id=1, source_target_pairs={{0,8},{8,0},{16,24},{24,16},{1,9},{9,1},{17,25},{25,17},{2,10},{10... | collective-permute-start | bytes 688136 | tf_op jit(solution)/shard_map/ppermute | solution.py:560
  6.4 12.0 %collective-permute-start.5 = (bf16[2,64,896]{2,1,0:T(8,128)(2,1)S(1)}, bf16[2,64,896]{2,1,0:T(8,128)(2,1)S(1)}, u32[]{:S(2)}, u32[]{:S(2)}) collective-permute-start(bf16[2,64,896]{2,1,0:T(8,128)(2,1)S(1)} %get-tuple-element.49), channel_id=1, source_target_pairs={{0,16},{8,24},{16,0},{24,8},{1,17},{9,25},{17,1},{25,9},{2,18},{10... | collective-permute-start | bytes 688136 | tf_op jit(solution)/shard_map/ppermute | solution.py:560
  8.0 10.5 %collective-permute-start.6 = (bf16[2,64,896]{2,1,0:T(8,128)(2,1)S(1)}, bf16[2,64,896]{2,1,0:T(8,128)(2,1)S(1)}, u32[]{:S(2)}, u32[]{:S(2)}) collective-permute-start(bf16[2,64,896]{2,1,0:T(8,128)(2,1)S(1)} %get-tuple-element.50), channel_id=1, source_target_pairs={{0,24},{8,16},{16,8},{24,0},{1,25},{9,17},{17,9},{25,1},{2,26},{10... | collective-permute-start | bytes 688136 | tf_op jit(solution)/shard_map/ppermute | solution.py:560
  21.1 28.7 %all-to-all-start.1 = ((bf16[8,64,896]{2,1,0:T(8,128)(2,1)}), bf16[8,64,896]{2,1,0:T(8,128)(2,1)S(1)}, u32[]{:S(2)}, u32[]{:S(2)}) async-start(bf16[8,64,896]{2,1,0:T(8,128)(2,1)} %bitcast.26), calls=%async_computation.1 | async-start | bytes 1835008 | tf_op jit(solution)/shard_map/all_to_all | solution.py:562
  30.3 11.0 %collective-permute-start.1 = (bf16[2,64,896]{2,1,0:T(8,128)(2,1)S(1)}, bf16[2,64,896]{2,1,0:T(8,128)(2,1)S(1)}, u32[]{:S(2)}, u32[]{:S(2)}) collective-permute-start(bf16[2,64,896]{2,1,0:T(8,128)(2,1)S(1)} %get-tuple-element.45), channel_id=1, source_target_pairs={{0,16},{8,24},{16,0},{24,8},{1,17},{9,25},{17,1},{25,9},{2,18},{10... | collective-permute-start | bytes 688136 | tf_op jit(solution)/shard_map/ppermute | solution.py:560
  31.1 11.8 %collective-permute-start.2 = (bf16[2,64,896]{2,1,0:T(8,128)(2,1)S(1)}, bf16[2,64,896]{2,1,0:T(8,128)(2,1)S(1)}, u32[]{:S(2)}, u32[]{:S(2)}) collective-permute-start(bf16[2,64,896]{2,1,0:T(8,128)(2,1)S(1)} %get-tuple-element.46), channel_id=1, source_target_pairs={{0,24},{8,16},{16,8},{24,0},{1,25},{9,17},{17,9},{25,1},{2,26},{10... | collective-permute-start | bytes 688136 | tf_op jit(solution)/shard_map/ppermute | solution.py:560
  49.8 27.3 %all-to-all-start = ((bf16[8,64,896]{2,1,0:T(8,128)(2,1)}), bf16[8,64,896]{2,1,0:T(8,128)(2,1)S(1)}, u32[]{:S(2)}, u32[]{:S(2)}) async-start(bf16[8,64,896]{2,1,0:T(8,128)(2,1)} %bitcast.23), calls=%async_computation | async-start | bytes 1835008 | tf_op jit(solution)/shard_map/all_to_all | solution.py:562
  65.4 16.3 %collective-permute-start.7 = (bf16[4,512,512]{2,1,0:T(8,128)(2,1)}, bf16[4,512,512]{2,1,0:T(8,128)(2,1)}, u32[]{:S(2)}, u32[]{:S(2)}) collective-permute-start(bf16[4,512,512]{2,1,0:T(8,128)(2,1)} %get-tuple-element.52), channel_id=1, source_target_pairs={{0,1},{1,0},{2,3},{3,2},{4,5},{5,4},{6,7},{7,6},{8,9},{9,8},{10,11... | collective-permute-start | bytes 6291464 | tf_op jit(solution)/shard_map/ppermute | solution.py:571
  84.9 9.5 %collective-permute-start.13 = (bf16[256,768]{1,0:T(8,128)(2,1)S(1)}, bf16[256,768]{1,0:T(8,128)(2,1)S(1)}, u32[]{:S(2)}, u32[]{:S(2)}) collective-permute-start(bf16[256,768]{1,0:T(8,128)(2,1)S(1)} %shard_map.115), channel_id=1, source_target_pairs={{0,2},{2,4},{4,6},{6,7},{7,5},{5,3},{3,1},{1,0},{8,10},{10,12},{12... | collective-permute-start | bytes 1179656 | tf_op jit(solution)/shard_map/ppermute | solution.py:608
  87.6 9.4 %collective-permute-start.10 = (bf16[2,512,256]{2,1,0:T(8,128)(2,1)S(1)}, bf16[2,512,256]{2,1,0:T(8,128)(2,1)S(1)}, u32[]{:S(2)}, u32[]{:S(2)}) collective-permute-start(bf16[2,512,256]{2,1,0:T(8,128)(2,1)S(1)} %shard_map.111), channel_id=1, source_target_pairs={{0,1},{1,0},{2,3},{3,2},{4,5},{5,4},{6,7},{7,6},{8,9},{9,8},{10,11... | collective-permute-start | bytes 1572872 | tf_op jit(solution)/shard_map/ppermute | solution.py:574
  90.2 9.8 %collective-permute-start.9 = (bf16[256,768]{1,0:T(8,128)(2,1)S(1)}, bf16[256,768]{1,0:T(8,128)(2,1)S(1)}, u32[]{:S(2)}, u32[]{:S(2)}) collective-permute-start(bf16[256,768]{1,0:T(8,128)(2,1)S(1)} %shard_map.110), channel_id=1, source_target_pairs={{0,2},{2,4},{4,6},{6,7},{7,5},{5,3},{3,1},{1,0},{8,10},{10,12},{12... | collective-permute-start | bytes 1179656 | tf_op jit(solution)/shard_map/ppermute | solution.py:608
  140.7 9.6 %collective-permute-start.23 = (bf16[256,768]{1,0:T(8,128)(2,1)S(1)}, bf16[256,768]{1,0:T(8,128)(2,1)S(1)}, u32[]{:S(2)}, u32[]{:S(2)}) collective-permute-start(bf16[256,768]{1,0:T(8,128)(2,1)S(1)} %collective-permute-done.21.refs_6_.refs_4_.refs_2_.refs_0_), channel_id=1, source_target_pairs={{0,2},{2,4},{4,6},{6,7},{7,5},{5,3},{3,1},{1,0},{8,10},{10,12},{12... | collective-permute-start | bytes 1179656 | tf_op jit(solution)/shard_map/ppermute | solution.py:608
  144.9 8.4 %collective-permute-start.24 = (bf16[256,768]{1,0:T(8,128)(2,1)S(1)}, bf16[256,768]{1,0:T(8,128)(2,1)S(1)}, u32[]{:S(2)}, u32[]{:S(2)}) collective-permute-start(bf16[256,768]{1,0:T(8,128)(2,1)S(1)} %collective-permute-done.22.refs_7_.refs_5_.refs_3_.refs_1_), channel_id=1, source_target_pairs={{0,2},{2,4},{4,6},{6,7},{7,5},{5,3},{3,1},{1,0},{8,10},{10,12},{12... | collective-permute-start | bytes 1179656 | tf_op jit(solution)/shard_map/ppermute | solution.py:608
  153.3 8.4 %collective-permute-start.26 = (bf16[256,768]{1,0:T(8,128)(2,1)S(1)}, bf16[256,768]{1,0:T(8,128)(2,1)S(1)}, u32[]{:S(2)}, u32[]{:S(2)}) collective-permute-start(bf16[256,768]{1,0:T(8,128)(2,1)S(1)} %collective-permute-done.24.refs_7_.refs_5_.refs_3_), channel_id=1, source_target_pairs={{0,2},{2,4},{4,6},{6,7},{7,5},{5,3},{3,1},{1,0},{8,10},{10,12},{12... | collective-permute-start | bytes 1179656 | tf_op jit(solution)/shard_map/ppermute | solution.py:608
  159.1 10.4 %collective-permute-start.27 = (bf16[256,768]{1,0:T(8,128)(2,1)S(1)}, bf16[256,768]{1,0:T(8,128)(2,1)S(1)}, u32[]{:S(2)}, u32[]{:S(2)}) collective-permute-start(bf16[256,768]{1,0:T(8,128)(2,1)S(1)} %shard_map.132), channel_id=1, source_target_pairs={{0,2},{2,4},{4,6},{6,7},{7,5},{5,3},{3,1},{1,0},{8,10},{10,12},{12... | collective-permute-start | bytes 1179656 | tf_op jit(solution)/shard_map/ppermute | solution.py:608
  161.7 8.4 %collective-permute-start.28 = (bf16[256,768]{1,0:T(8,128)(2,1)S(1)}, bf16[256,768]{1,0:T(8,128)(2,1)S(1)}, u32[]{:S(2)}, u32[]{:S(2)}) collective-permute-start(bf16[256,768]{1,0:T(8,128)(2,1)S(1)} %collective-permute-done.26.refs_7_.refs_5_), channel_id=1, source_target_pairs={{0,2},{2,4},{4,6},{6,7},{7,5},{5,3},{3,1},{1,0},{8,10},{10,12},{12... | collective-permute-start | bytes 1179656 | tf_op jit(solution)/shard_map/ppermute | solution.py:608
  180.4 12.7 %collective-permute-start.33 = (bf16[64,896]{1,0:T(8,128)(2,1)S(1)}, bf16[64,896]{1,0:T(8,128)(2,1)S(1)}, u32[]{:S(2)}, u32[]{:S(2)}) collective-permute-start(bf16[64,896]{1,0:T(8,128)(2,1)S(1)} %get-tuple-element.61), channel_id=1, source_target_pairs={{0,0},{8,1},{16,2},{24,3},{1,4},{9,5},{17,6},{25,7},{2,8},{10,9},{... | collective-permute-start | bytes 344072 | tf_op jit(solution)/shard_map/ppermute | solution.py:630
  181.1 16.7 %collective-permute-start.34 = (bf16[64,896]{1,0:T(8,128)(2,1)S(1)}, bf16[64,896]{1,0:T(8,128)(2,1)S(1)}, u32[]{:S(2)}, u32[]{:S(2)}) collective-permute-start(bf16[64,896]{1,0:T(8,128)(2,1)S(1)} %get-tuple-element.62), channel_id=1, source_target_pairs={{8,0},{0,1},{24,2},{16,3},{9,4},{1,5},{25,6},{17,7},{10,8},{2,9},{... | collective-permute-start | bytes 344072 | tf_op jit(solution)/shard_map/ppermute | solution.py:630
  184.4 15.4 %collective-permute-start.35 = (bf16[64,896]{1,0:T(8,128)(2,1)S(1)}, bf16[64,896]{1,0:T(8,128)(2,1)S(1)}, u32[]{:S(2)}, u32[]{:S(2)}) collective-permute-start(bf16[64,896]{1,0:T(8,128)(2,1)S(1)} %get-tuple-element.63), channel_id=1, source_target_pairs={{16,0},{24,1},{0,2},{8,3},{17,4},{25,5},{1,6},{9,7},{18,8},{26,9},... | collective-permute-start | bytes 344072 | tf_op jit(solution)/shard_map/ppermute | solution.py:630
  186.6 24.6 %collective-permute-start.36 = (bf16[64,896]{1,0:T(8,128)(2,1)S(1)}, bf16[64,896]{1,0:T(8,128)(2,1)S(1)}, u32[]{:S(2)}, u32[]{:S(2)}) collective-permute-start(bf16[64,896]{1,0:T(8,128)(2,1)S(1)} %get-tuple-element.64), channel_id=1, source_target_pairs={{24,0},{16,1},{8,2},{0,3},{25,4},{17,5},{9,6},{1,7},{26,8},{18,9},... | collective-permute-start | bytes 344072 | tf_op jit(solution)/shard_map/ppermute | solution.py:630
  191.4 19.8 %collective-permute-start.37 = (bf16[64,896]{1,0:T(8,128)(2,1)S(1)}, bf16[64,896]{1,0:T(8,128)(2,1)S(1)}, u32[]{:S(2)}, u32[]{:S(2)}) collective-permute-start(bf16[64,896]{1,0:T(8,128)(2,1)S(1)} %get-tuple-element.65), channel_id=1, source_target_pairs={{1,0},{9,1},{17,2},{25,3},{0,4},{8,5},{16,6},{24,7},{3,8},{11,9},{... | collective-permute-start | bytes 344072 | tf_op jit(solution)/shard_map/ppermute | solution.py:630
  193.2 18.1 %collective-permute-start.38 = (bf16[64,896]{1,0:T(8,128)(2,1)S(1)}, bf16[64,896]{1,0:T(8,128)(2,1)S(1)}, u32[]{:S(2)}, u32[]{:S(2)}) collective-permute-start(bf16[64,896]{1,0:T(8,128)(2,1)S(1)} %get-tuple-element.66), channel_id=1, source_target_pairs={{9,0},{1,1},{25,2},{17,3},{8,4},{0,5},{24,6},{16,7},{11,8},{3,9},{... | collective-permute-start | bytes 344072 | tf_op jit(solution)/shard_map/ppermute | solution.py:630
  197.8 13.4 %collective-permute-start.39 = (bf16[64,896]{1,0:T(8,128)(2,1)S(1)}, bf16[64,896]{1,0:T(8,128)(2,1)S(1)}, u32[]{:S(2)}, u32[]{:S(2)}) collective-permute-start(bf16[64,896]{1,0:T(8,128)(2,1)S(1)} %get-tuple-element.67), channel_id=1, source_target_pairs={{17,0},{25,1},{1,2},{9,3},{16,4},{24,5},{0,6},{8,7},{19,8},{27,9},... | collective-permute-start | bytes 344072 | tf_op jit(solution)/shard_map/ppermute | solution.py:630
  199.8 11.5 %collective-permute-start.40 = (bf16[64,896]{1,0:T(8,128)(2,1)S(1)}, bf16[64,896]{1,0:T(8,128)(2,1)S(1)}, u32[]{:S(2)}, u32[]{:S(2)}) collective-permute-start(bf16[64,896]{1,0:T(8,128)(2,1)S(1)} %get-tuple-element.68), channel_id=1, source_target_pairs={{25,0},{17,1},{9,2},{1,3},{24,4},{16,5},{8,6},{0,7},{27,8},{19,9},... | collective-permute-start | bytes 344072 | tf_op jit(solution)/shard_map/ppermute | solution.py:630
  (30 other events, 169.8 us)
where the time goes:
time: 217 us; the launch traced here: 216 us
  starting transfers between devices  82.8 us (38%)
  waiting for transfers between devices  64.8 us (30%)
  Pallas kernels  64.2 us (30%)
  local copies, waits for them, and re-layouts  2.8 us (1%)
    ppermute x20, starting transfers between devices, body(): came.append(lax.ppermute(send, 'dp', ring))  41.5 us
    ppermute x20, waiting for transfers between devices, body(): came.append(lax.ppermute(send, 'dp', ring))  24.6 us
    ppermute x8, starting transfers between devices, body(): returned.append(lax.ppermute(piece, ('expert', 'dp'), pairs))  21.7 us
    ppermute x6, waiting for transfers between devices, exchange(): lax.ppermute(messages[t], 'expert', [(q, q ^ t) for q in range(experts)])  20.8 us
    all_to_all x2, waiting for transfers between devices, exchange(): lax.all_to_all(blocks, 'dp', split_axis=0, concat_axis=0, tiled=True)  15.5 us
    pallas_call x4, Pallas kernels, gradients(): pl.pallas_call(functools.partial(gradients_kernel, units, scale, grads is...  13.6 us
    pallas_call x4, Pallas kernels, back_rows(): pl.pallas_call(back_kernel, out_shape=jax.ShapeDtypeStruct((size, slots,...  11.3 us
    pallas_call x1, Pallas kernels, gate_up(): pl.pallas_call(gate_up_kernel, out_shape=(out, out, jax.ShapeDtypeStruct(...  10.7 us
  transfers between devices with their start and end apart: 43, of which 25 were waited for; matrix products, arithmetic and copies ran while one was open for 0% of the time, Pallas kernels for 21%

commit v1 on v0

--- a/solution.py
+++ b/solution.py
@@ -197,7 +197,7 @@
         ),
         compiler_params=PARAMS,
         cost_estimate=cost(),
-    )(scalars, *in_hbm(hot, *pieces))
+    )(scalars, hot, *in_hbm(*pieces))
     if feats % 128:
         out = out.transpose(1, 0, 2).reshape(tokens, 2 * feats)
     return out
@@ -613,13 +613,11 @@
     others = [lax.ppermute(message, "dp", swap) for message in mine]
     acc, token = sum_rows(scalars, 0, mine, gate_and_up, None, 0)
     last = pick(token, early, count - early)
-    grads, _ = gradients(
-        token, ready, count, inv_root, x_t, g, mine[ready:], grads
-    )
-    mine = last
-    others += [lax.ppermute(message, "dp", swap) for message in mine]
-    units = [*mine, *others]
-    pieces = sum_rows(scalars, early, units, gate_and_up, acc, groups)
+    mine += last
+    others += [lax.ppermute(message, "dp", swap) for message in last]
+    grads, token = gradients(token, ready, count, inv_root, x_t, g, mine[ready:], grads)
+    units = [*last, *others]
+    pieces = sum_rows(token, early, units, gate_and_up, acc, groups)
     returned = []
     for r, piece in enumerate(pieces):
         pairs = []
@@ -628,7 +626,7 @@
                 h, e = divmod(b ^ r, experts)
                 pairs.append((e * groups + 2 * q + h, q * groups + b))
         returned.append(lax.ppermute(piece, ("expert", "dp"), pairs))
-    grads, _ = gradients(scalars, early, count, inv_root, x_t, g, units, grads)
+    grads, _ = gradients(scalars, count, count, inv_root, x_t, g, others, grads)
     grad_tokens = combine_rows(scalars, hot, returned, experts)
     return (grad_tokens, grads[0][None], grads[1][None], grads[2][None])
 

time: 217 us -> 216 us (level)
  transfers between devices with their start and end apart: 43 -> 43, of which waited for: 25 -> 24; matrix products, arithmetic and copies ran while one was open for 0% -> 0% of each run, Pallas kernels for 21% -> 22%
where the time goes in v1:
time: 216 us; the launch traced here: 214 us
  starting transfers between devices  82.8 us (38%)
  Pallas kernels  63.6 us (29%)
  waiting for transfers between devices  63.4 us (29%)
  local copies, waits for them, and re-layouts  2.18 us (1%)
    ppermute x20, starting transfers between devices, body(): came.append(lax.ppermute(send, 'dp', ring))  41.5 us
    ppermute x20, waiting for transfers between devices, body(): came.append(lax.ppermute(send, 'dp', ring))  24.6 us
    ppermute x8, starting transfers between devices, body(): returned.append(lax.ppermute(piece, ('expert', 'dp'), pairs))  21.7 us
    ppermute x6, waiting for transfers between devices, exchange(): lax.ppermute(messages[t], 'expert', [(q, q ^ t) for q in range(experts)])  20.8 us
    all_to_all x2, waiting for transfers between devices, exchange(): lax.all_to_all(blocks, 'dp', split_axis=0, concat_axis=0, tiled=True)  16.1 us
    pallas_call x4, Pallas kernels, gradients(): pl.pallas_call(functools.partial(gradients_kernel, units, scale, grads is...  13.8 us
    pallas_call x4, Pallas kernels, back_rows(): pl.pallas_call(back_kernel, out_shape=jax.ShapeDtypeStruct((size, slots,...  11.3 us
    pallas_call x1, Pallas kernels, gate_up(): pl.pallas_call(gate_up_kernel, out_shape=(out, out, jax.ShapeDtypeStruct(...  10.7 us
  transfers between devices with their start and end apart: 43, of which 24 were waited for; matrix products, arithmetic and copies ran while one was open for 0% of the time, Pallas kernels for 22%

profile of v1, /device:TPU:0, one launch (start us, length us, event | category | flops | bytes accessed | tf_op | source)
XLA Modules:
  0.0 213.5 jit_solution(8610604915200480246)
XLA Ops:
  3.4 3.0 %collective-permute-start.4 = (bf16[2,64,896]{2,1,0:T(8,128)(2,1)S(1)}, bf16[2,64,896]{2,1,0:T(8,128)(2,1)S(1)}, u32[]{:S(2)}, u32[]{:S(2)}) collective-permute-start(bf16[2,64,896]{2,1,0:T(8,128)(2,1)S(1)} %get-tuple-element.49), channel_id=1, source_target_pairs={{0,8},{8,0},{16,24},{24,16},{1,9},{9,1},{17,25},{25,17},{2,10},{10... | collective-permute-start | bytes 688136 | tf_op jit(solution)/shard_map/ppermute | solution.py:560
  8.0 4.9 %collective-permute-done.4.refs_1_ = bf16[2,64,896]{2,1,0:T(8,128)(2,1)S(1)} collective-permute-done((bf16[2,64,896]{2,1,0:T(8,128)(2,1)S(1)}, bf16[2,64,896]{2,1,0:T(8,128)(2,1)S(1)}, u32[]{:S(2)}, u32[]{:S(2)}) %collective-permute-start.4) | collective-permute-done | bytes 229408 | tf_op jit(solution)/shard_map/ppermute | solution.py:560
  12.9 5.5 %collective-permute-done.5.refs_2_ = bf16[2,64,896]{2,1,0:T(8,128)(2,1)S(1)} collective-permute-done((bf16[2,64,896]{2,1,0:T(8,128)(2,1)S(1)}, bf16[2,64,896]{2,1,0:T(8,128)(2,1)S(1)}, u32[]{:S(2)}, u32[]{:S(2)}) %collective-permute-start.5) | collective-permute-done | bytes 229408 | tf_op jit(solution)/shard_map/ppermute | solution.py:560
  18.4 2.7 %shard_map.106 = bf16[4,2,64,896]{3,2,1,0:T(8,128)(2,1)} custom-call(s32[21]{0:T(128)S(1)} %stack.87.scalar_ref, bf16[2,64,896]{2,1,0:T(8,128)(2,1)S(1)} %get-tuple-element.48.refs_0_, bf16[2,64,896]{2,1,0:T(8,128)(2,1)S(1)} %collective-permute-done.4.refs_1_, bf16[2,64,896]{2,1,0:T(8,128)(2,1)S(1)} %collective-permute-done.5.refs_2_, ...), custom_call_target="tpu_custom_call" | custom-call | flops 1024 | bytes 1024 | tf_op jit(solution)/shard_map/pallas_call | solution.py:131
  21.1 4.9 %all-to-all-start.1 = ((bf16[8,64,896]{2,1,0:T(8,128)(2,1)}), bf16[8,64,896]{2,1,0:T(8,128)(2,1)S(1)}, u32[]{:S(2)}, u32[]{:S(2)}) async-start(bf16[8,64,896]{2,1,0:T(8,128)(2,1)} %bitcast.26), calls=%async_computation.1 | async-start | bytes 1835008 | tf_op jit(solution)/shard_map/all_to_all | solution.py:562
  31.9 4.9 %collective-permute-done.refs_1_ = bf16[2,64,896]{2,1,0:T(8,128)(2,1)S(1)} collective-permute-done((bf16[2,64,896]{2,1,0:T(8,128)(2,1)S(1)}, bf16[2,64,896]{2,1,0:T(8,128)(2,1)S(1)}, u32[]{:S(2)}, u32[]{:S(2)}) %collective-permute-start) | collective-permute-done | bytes 229408 | tf_op jit(solution)/shard_map/ppermute | solution.py:560
  36.9 3.9 %collective-permute-done.1.refs_2_ = bf16[2,64,896]{2,1,0:T(8,128)(2,1)S(1)} collective-permute-done((bf16[2,64,896]{2,1,0:T(8,128)(2,1)S(1)}, bf16[2,64,896]{2,1,0:T(8,128)(2,1)S(1)}, u32[]{:S(2)}, u32[]{:S(2)}) %collective-permute-start.1) | collective-permute-done | bytes 229408 | tf_op jit(solution)/shard_map/ppermute | solution.py:560
  42.3 2.7 %shard_map.104 = bf16[4,2,64,896]{3,2,1,0:T(8,128)(2,1)} custom-call(s32[21]{0:T(128)S(1)} %stack.87.scalar_ref, bf16[2,64,896]{2,1,0:T(8,128)(2,1)S(1)} %get-tuple-element.44.refs_0_, bf16[2,64,896]{2,1,0:T(8,128)(2,1)S(1)} %collective-permute-done.refs_1_, bf16[2,64,896]{2,1,0:T(8,128)(2,1)S(1)} %collective-permute-done.1.refs_2_, ...), custom_call_target="tpu_custom_call" | custom-call | flops 1024 | bytes 1024 | tf_op jit(solution)/shard_map/pallas_call | solution.py:131
  45.0 4.8 %all-to-all-done.1 = bf16[8,64,896]{2,1,0:T(8,128)(2,1)S(1)} async-done(((bf16[8,64,896]{2,1,0:T(8,128)(2,1)}), bf16[8,64,896]{2,1,0:T(8,128)(2,1)S(1)}, u32[]{:S(2)}, u32[]{:S(2)}) %all-to-all-start.1) | async-done | bytes 917536 | tf_op jit(solution)/shard_map/all_to_all | solution.py:562
  49.8 3.6 %all-to-all-start = ((bf16[8,64,896]{2,1,0:T(8,128)(2,1)}), bf16[8,64,896]{2,1,0:T(8,128)(2,1)S(1)}, u32[]{:S(2)}, u32[]{:S(2)}) async-start(bf16[8,64,896]{2,1,0:T(8,128)(2,1)} %bitcast.23), calls=%async_computation | async-start | bytes 1835008 | tf_op jit(solution)/shard_map/all_to_all | solution.py:562
  53.4 10.7 %shard_map.107 = (bf16[4,512,512]{2,1,0:T(8,128)(2,1)}, bf16[4,512,512]{2,1,0:T(8,128)(2,1)S(1)}, bf16[896,512]{1,0:T(8,128)(2,1)S(1)}) custom-call(s32[21]{0:T(128)S(1)} %stack.87.scalar_ref, bf16[512,896]{1,0:T(8,128)(2,1)S(1)} %bitcast.41, bf16[896,2048]{1,0:T(8,128)(2,1)} %bitcast.42, bf16[896,2048]{1,0:T(8,128)(2,1)} %bitcast.51), custom_call_target="tpu_custom_call" | custom-call | flops 1024 | bytes 1024 | tf_op jit(solution)/shard_map/pallas_call | solution.py:229
  65.8 11.3 %all-to-all-done = bf16[8,64,896]{2,1,0:T(8,128)(2,1)S(1)} async-done(((bf16[8,64,896]{2,1,0:T(8,128)(2,1)}), bf16[8,64,896]{2,1,0:T(8,128)(2,1)S(1)}, u32[]{:S(2)}, u32[]{:S(2)}) %all-to-all-start) | async-done | bytes 917536 | tf_op jit(solution)/shard_map/all_to_all | solution.py:562
  77.1 2.6 %shard_map.105 = bf16[2,512,256]{2,1,0:T(8,128)(2,1)S(1)} custom-call(s32[21]{0:T(128)S(1)} %stack.87.scalar_ref, bf16[512,896]{1,0:T(8,128)(2,1)S(1)} %bitcast.33, bf16[2048,896]{1,0:T(8,128)(2,1)} %bitcast.60), custom_call_target="tpu_custom_call" | custom-call | flops 1024 | bytes 1024 | tf_op jit(solution)/shard_map/pallas_call | solution.py:272
  81.7 3.1 %shard_map.108.refs_0_.refs_1_ = bf16[2,512,768]{2,1,0:T(8,128)(2,1)S(1)} custom-call(s32[21]{0:T(128)S(1)} %stack.87.scalar_ref, bf16[512,896]{1,0:T(8,128)(2,1)S(1)} %bitcast.34, bf16[2048,896]{1,0:T(8,128)(2,1)} %bitcast.61, bf16[2,512,256]{2,1,0:T(8,128)(2,1)S(1)} %collective-permute-done.3.refs_0_, bf16[4,512,512]{2,1,0:T(8,128)(2,1)S(1)} %copy-done.1, ...), custom_call_target="tpu_custom_call" | custom-call | flops 1024 | bytes 1024 | tf_op jit(solution)/shard_map/pallas_call | solution.py:272
  97.0 3.1 %shard_map.112.refs_1_ = bf16[2,512,768]{2,1,0:T(8,128)(2,1)S(1)} custom-call(s32[21]{0:T(128)S(1)} %stack.87.scalar_ref, bf16[512,896]{1,0:T(8,128)(2,1)S(1)} %bitcast.36, bf16[2048,896]{1,0:T(8,128)(2,1)} %bitcast.63, bf16[2,512,256]{2,1,0:T(8,128)(2,1)S(1)} %collective-permute-done.10.refs_0_, bf16[4,512,512]{2,1,0:T(8,128)(2,1)S(1)} %copy-done.1, ...), custom_call_target="tpu_custom_call" | custom-call | flops 1024 | bytes 1024 | tf_op jit(solution)/shard_map/pallas_call | solution.py:272
  165.2 4.2 %shard_map.130 = (f32[512,896]{1,0:T(8,128)S(1)}, s32[21]{0:T(128)S(1)}) custom-call(s32[21]{0:T(128)S(1)} %stack.87.scalar_ref, bf16[512,768]{1,0:T(8,128)(2,1)S(1)} %shard_map.125.refs_0_, bf16[512,768]{1,0:T(8,128)(2,1)S(1)} %shard_map.126.refs_1_.refs_0_, bf16[512,768]{1,0:T(8,128)(2,1)S(1)} %shard_map.129.refs_2_.refs_0_, bf16[896,2048]{1,0:T(8,128)(2,1)} %bitcast.43, ...), custom_call_target="tpu_custom_call" | custom-call | flops 1024 | bytes 1024 | tf_op jit(solution)/shard_map/pallas_call | solution.py:514
  172.6 3.6 %shard_map.134 = (bf16[896,2048]{1,0:T(8,128)(2,1)}, bf16[896,2048]{1,0:T(8,128)(2,1)}, bf16[2048,896]{1,0:T(8,128)(2,1)}, s32[21]{0:T(128)S(1)}) custom-call(s32[21]{0:T(128)S(1)} %get-tuple-element.56.scalar_ref, bf16[896,512]{1,0:T(8,128)(2,1)S(1)} %get-tuple-element.54.xt_ref, ...), custom_call_target="tpu_custom_call", output_to_operand_aliasing={{0}: (5, {}), {1}: (6, {}), {2}: (7, {})} | custom-call | flops 1024 | bytes 1024 | tf_op jit(solution)/shard_map/pallas_call | solution.py:446
  176.3 5.9 %shard_map.135 = (bf16[64,896]{1,0:T(8,128)(2,1)S(1)}, bf16[64,896]{1,0:T(8,128)(2,1)S(1)}, bf16[64,896]{1,0:T(8,128)(2,1)S(1)}, bf16[64,896]{1,0:T(8,128)(2,1)S...) custom-call(s32[21]{0:T(128)S(1)} %get-tuple-element.64.scalar_ref, ...), custom_call_target="tpu_custom_call" | custom-call | flops 1024 | bytes 1024 | tf_op jit(solution)/shard_map/pallas_call | solution.py:514
  182.9 2.9 %collective-permute-start.34 = (bf16[64,896]{1,0:T(8,128)(2,1)S(1)}, bf16[64,896]{1,0:T(8,128)(2,1)S(1)}, u32[]{:S(2)}, u32[]{:S(2)}) collective-permute-start(bf16[64,896]{1,0:T(8,128)(2,1)S(1)} %get-tuple-element.67), channel_id=1, source_target_pairs={{8,0},{0,1},{24,2},{16,3},{9,4},{1,5},{25,6},{17,7},{10,8},{2,9},{... | collective-permute-start | bytes 344072 | tf_op jit(solution)/shard_map/ppermute | solution.py:628
  185.7 2.6 %collective-permute-start.35 = (bf16[64,896]{1,0:T(8,128)(2,1)S(1)}, bf16[64,896]{1,0:T(8,128)(2,1)S(1)}, u32[]{:S(2)}, u32[]{:S(2)}) collective-permute-start(bf16[64,896]{1,0:T(8,128)(2,1)S(1)} %get-tuple-element.68), channel_id=1, source_target_pairs={{16,0},{24,1},{0,2},{8,3},{17,4},{25,5},{1,6},{9,7},{18,8},{26,9},... | collective-permute-start | bytes 344072 | tf_op jit(solution)/shard_map/ppermute | solution.py:628
  188.4 4.7 %collective-permute-start.36 = (bf16[64,896]{1,0:T(8,128)(2,1)S(1)}, bf16[64,896]{1,0:T(8,128)(2,1)S(1)}, u32[]{:S(2)}, u32[]{:S(2)}) collective-permute-start(bf16[64,896]{1,0:T(8,128)(2,1)S(1)} %get-tuple-element.69), channel_id=1, source_target_pairs={{24,0},{16,1},{8,2},{0,3},{25,4},{17,5},{9,6},{1,7},{26,8},{18,9},... | collective-permute-start | bytes 344072 | tf_op jit(solution)/shard_map/ppermute | solution.py:628
  194.6 5.0 %collective-permute-start.38 = (bf16[64,896]{1,0:T(8,128)(2,1)S(1)}, bf16[64,896]{1,0:T(8,128)(2,1)S(1)}, u32[]{:S(2)}, u32[]{:S(2)}) collective-permute-start(bf16[64,896]{1,0:T(8,128)(2,1)S(1)} %get-tuple-element.71), channel_id=1, source_target_pairs={{9,0},{1,1},{25,2},{17,3},{8,4},{0,5},{24,6},{16,7},{11,8},{3,9},{... | collective-permute-start | bytes 344072 | tf_op jit(solution)/shard_map/ppermute | solution.py:628
  204.0 5.6 %shard_map.137 = (bf16[896,2048]{1,0:T(8,128)(2,1)}, bf16[896,2048]{1,0:T(8,128)(2,1)}, bf16[2048,896]{1,0:T(8,128)(2,1)}, s32[21]{0:T(128)}) custom-call(s32[21]{0:T(128)S(1)} %stack.87.scalar_ref, bf16[896,512]{1,0:T(8,128)(2,1)S(1)} %get-tuple-element.54.xt_ref, ...), custom_call_target="tpu_custom_call", output_to_operand_aliasing={{0}: (7, {}), {1}: (8, {}), {2}: (9, {})} | custom-call | flops 1024 | bytes 1024 | tf_op jit(solution)/shard_map/pallas_call | solution.py:446
  210.4 2.9 %shard_map.136 = bf16[128,1792]{1,0:T(8,128)(2,1)} custom-call(s32[21]{0:T(128)S(1)} %stack.87.scalar_ref, bf16[256,128]{1,0:T(8,128)(2,1)S(1)} %get-tuple-element.43.hot_ref, bf16[64,896]{1,0:T(8,128)(2,1)} %copy-done.2, bf16[64,896]{1,0:T(8,128)(2,1)} %copy-done.3, bf16[64,896]{1,0:T(8,128)(2,1)} %copy-done.4, bf16[64,896]{1,0:T(8,128)(2,1)} %copy-done.5, ...), custom_call_target="tpu_custom_call" | custom-call | flops 1024 | bytes 1024 | tf_op jit(solution)/shard_map/pallas_call | solution.py:184
  (119 shorter events, 103.0 us)
Async XLA Ops:
  3.4 9.4 %collective-permute-start.4 = (bf16[2,64,896]{2,1,0:T(8,128)(2,1)S(1)}, bf16[2,64,896]{2,1,0:T(8,128)(2,1)S(1)}, u32[]{:S(2)}, u32[]{:S(2)}) collective-permute-start(bf16[2,64,896]{2,1,0:T(8,128)(2,1)S(1)} %get-tuple-element.49), channel_id=1, source_target_pairs={{0,8},{8,0},{16,24},{24,16},{1,9},{9,1},{17,25},{25,17},{2,10},{10... | collective-permute-start | bytes 688136 | tf_op jit(solution)/shard_map/ppermute | solution.py:560
  6.4 12.0 %collective-permute-start.5 = (bf16[2,64,896]{2,1,0:T(8,128)(2,1)S(1)}, bf16[2,64,896]{2,1,0:T(8,128)(2,1)S(1)}, u32[]{:S(2)}, u32[]{:S(2)}) collective-permute-start(bf16[2,64,896]{2,1,0:T(8,128)(2,1)S(1)} %get-tuple-element.50), channel_id=1, source_target_pairs={{0,16},{8,24},{16,0},{24,8},{1,17},{9,25},{17,1},{25,9},{2,18},{10... | collective-permute-start | bytes 688136 | tf_op jit(solution)/shard_map/ppermute | solution.py:560
  7.9 10.5 %collective-permute-start.6 = (bf16[2,64,896]{2,1,0:T(8,128)(2,1)S(1)}, bf16[2,64,896]{2,1,0:T(8,128)(2,1)S(1)}, u32[]{:S(2)}, u32[]{:S(2)}) collective-permute-start(bf16[2,64,896]{2,1,0:T(8,128)(2,1)S(1)} %get-tuple-element.51), channel_id=1, source_target_pairs={{0,24},{8,16},{16,8},{24,0},{1,25},{9,17},{17,9},{25,1},{2,26},{10... | collective-permute-start | bytes 688136 | tf_op jit(solution)/shard_map/ppermute | solution.py:560
  21.1 28.7 %all-to-all-start.1 = ((bf16[8,64,896]{2,1,0:T(8,128)(2,1)}), bf16[8,64,896]{2,1,0:T(8,128)(2,1)S(1)}, u32[]{:S(2)}, u32[]{:S(2)}) async-start(bf16[8,64,896]{2,1,0:T(8,128)(2,1)} %bitcast.26), calls=%async_computation.1 | async-start | bytes 1835008 | tf_op jit(solution)/shard_map/all_to_all | solution.py:562
  28.4 8.5 %collective-permute-start = (bf16[2,64,896]{2,1,0:T(8,128)(2,1)S(1)}, bf16[2,64,896]{2,1,0:T(8,128)(2,1)S(1)}, u32[]{:S(2)}, u32[]{:S(2)}) collective-permute-start(bf16[2,64,896]{2,1,0:T(8,128)(2,1)S(1)} %get-tuple-element.45), channel_id=1, source_target_pairs={{0,8},{8,0},{16,24},{24,16},{1,9},{9,1},{17,25},{25,17},{2,10},{10... | collective-permute-start | bytes 688136 | tf_op jit(solution)/shard_map/ppermute | solution.py:560
  29.7 11.0 %collective-permute-start.1 = (bf16[2,64,896]{2,1,0:T(8,128)(2,1)S(1)}, bf16[2,64,896]{2,1,0:T(8,128)(2,1)S(1)}, u32[]{:S(2)}, u32[]{:S(2)}) collective-permute-start(bf16[2,64,896]{2,1,0:T(8,128)(2,1)S(1)} %get-tuple-element.46), channel_id=1, source_target_pairs={{0,16},{8,24},{16,0},{24,8},{1,17},{9,25},{17,1},{25,9},{2,18},{10... | collective-permute-start | bytes 688136 | tf_op jit(solution)/shard_map/ppermute | solution.py:560
  30.5 11.8 %collective-permute-start.2 = (bf16[2,64,896]{2,1,0:T(8,128)(2,1)S(1)}, bf16[2,64,896]{2,1,0:T(8,128)(2,1)S(1)}, u32[]{:S(2)}, u32[]{:S(2)}) collective-permute-start(bf16[2,64,896]{2,1,0:T(8,128)(2,1)S(1)} %get-tuple-element.47), channel_id=1, source_target_pairs={{0,24},{8,16},{16,8},{24,0},{1,25},{9,17},{17,9},{25,1},{2,26},{10... | collective-permute-start | bytes 688136 | tf_op jit(solution)/shard_map/ppermute | solution.py:560
  49.8 27.3 %all-to-all-start = ((bf16[8,64,896]{2,1,0:T(8,128)(2,1)}), bf16[8,64,896]{2,1,0:T(8,128)(2,1)S(1)}, u32[]{:S(2)}, u32[]{:S(2)}) async-start(bf16[8,64,896]{2,1,0:T(8,128)(2,1)} %bitcast.23), calls=%async_computation | async-start | bytes 1835008 | tf_op jit(solution)/shard_map/all_to_all | solution.py:562
  65.4 16.3 %collective-permute-start.7 = (bf16[4,512,512]{2,1,0:T(8,128)(2,1)}, bf16[4,512,512]{2,1,0:T(8,128)(2,1)}, u32[]{:S(2)}, u32[]{:S(2)}) collective-permute-start(bf16[4,512,512]{2,1,0:T(8,128)(2,1)} %get-tuple-element.53), channel_id=1, source_target_pairs={{0,1},{1,0},{2,3},{3,2},{4,5},{5,4},{6,7},{7,6},{8,9},{9,8},{10,11... | collective-permute-start | bytes 6291464 | tf_op jit(solution)/shard_map/ppermute | solution.py:571
  84.9 9.5 %collective-permute-start.13 = (bf16[256,768]{1,0:T(8,128)(2,1)S(1)}, bf16[256,768]{1,0:T(8,128)(2,1)S(1)}, u32[]{:S(2)}, u32[]{:S(2)}) collective-permute-start(bf16[256,768]{1,0:T(8,128)(2,1)S(1)} %shard_map.115), channel_id=1, source_target_pairs={{0,2},{2,4},{4,6},{6,7},{7,5},{5,3},{3,1},{1,0},{8,10},{10,12},{12... | collective-permute-start | bytes 1179656 | tf_op jit(solution)/shard_map/ppermute | solution.py:608
  87.6 9.4 %collective-permute-start.10 = (bf16[2,512,256]{2,1,0:T(8,128)(2,1)S(1)}, bf16[2,512,256]{2,1,0:T(8,128)(2,1)S(1)}, u32[]{:S(2)}, u32[]{:S(2)}) collective-permute-start(bf16[2,512,256]{2,1,0:T(8,128)(2,1)S(1)} %shard_map.111), channel_id=1, source_target_pairs={{0,1},{1,0},{2,3},{3,2},{4,5},{5,4},{6,7},{7,6},{8,9},{9,8},{10,11... | collective-permute-start | bytes 1572872 | tf_op jit(solution)/shard_map/ppermute | solution.py:574
  90.2 9.8 %collective-permute-start.9 = (bf16[256,768]{1,0:T(8,128)(2,1)S(1)}, bf16[256,768]{1,0:T(8,128)(2,1)S(1)}, u32[]{:S(2)}, u32[]{:S(2)}) collective-permute-start(bf16[256,768]{1,0:T(8,128)(2,1)S(1)} %shard_map.110), channel_id=1, source_target_pairs={{0,2},{2,4},{4,6},{6,7},{7,5},{5,3},{3,1},{1,0},{8,10},{10,12},{12... | collective-permute-start | bytes 1179656 | tf_op jit(solution)/shard_map/ppermute | solution.py:608
  140.7 9.6 %collective-permute-start.23 = (bf16[256,768]{1,0:T(8,128)(2,1)S(1)}, bf16[256,768]{1,0:T(8,128)(2,1)S(1)}, u32[]{:S(2)}, u32[]{:S(2)}) collective-permute-start(bf16[256,768]{1,0:T(8,128)(2,1)S(1)} %collective-permute-done.21.refs_6_.refs_4_.refs_2_.refs_0_), channel_id=1, source_target_pairs={{0,2},{2,4},{4,6},{6,7},{7,5},{5,3},{3,1},{1,0},{8,10},{10,12},{12... | collective-permute-start | bytes 1179656 | tf_op jit(solution)/shard_map/ppermute | solution.py:608
  144.9 8.4 %collective-permute-start.24 = (bf16[256,768]{1,0:T(8,128)(2,1)S(1)}, bf16[256,768]{1,0:T(8,128)(2,1)S(1)}, u32[]{:S(2)}, u32[]{:S(2)}) collective-permute-start(bf16[256,768]{1,0:T(8,128)(2,1)S(1)} %collective-permute-done.22.refs_7_.refs_5_.refs_3_.refs_1_), channel_id=1, source_target_pairs={{0,2},{2,4},{4,6},{6,7},{7,5},{5,3},{3,1},{1,0},{8,10},{10,12},{12... | collective-permute-start | bytes 1179656 | tf_op jit(solution)/shard_map/ppermute | solution.py:608
  159.1 10.4 %collective-permute-start.27 = (bf16[256,768]{1,0:T(8,128)(2,1)S(1)}, bf16[256,768]{1,0:T(8,128)(2,1)S(1)}, u32[]{:S(2)}, u32[]{:S(2)}) collective-permute-start(bf16[256,768]{1,0:T(8,128)(2,1)S(1)} %shard_map.132), channel_id=1, source_target_pairs={{0,2},{2,4},{4,6},{6,7},{7,5},{5,3},{3,1},{1,0},{8,10},{10,12},{12... | collective-permute-start | bytes 1179656 | tf_op jit(solution)/shard_map/ppermute | solution.py:608
  164.2 12.0 %collective-permute-start.29 = (bf16[512,768]{1,0:T(8,128)(2,1)S(1)}, bf16[512,768]{1,0:T(8,128)(2,1)S(1)}, u32[]{:S(2)}, u32[]{:S(2)}) collective-permute-start(bf16[512,768]{1,0:T(8,128)(2,1)S(1)} %shard_map.125.refs_0_), channel_id=1, source_target_pairs={{0,1},{1,0},{2,3},{3,2},{4,5},{5,4},{6,7},{7,6},{8,9},{9,8},{10,11... | collective-permute-start | bytes 2359304 | tf_op jit(solution)/shard_map/ppermute | solution.py:613
  164.6 11.6 %collective-permute-start.30 = (bf16[512,768]{1,0:T(8,128)(2,1)S(1)}, bf16[512,768]{1,0:T(8,128)(2,1)S(1)}, u32[]{:S(2)}, u32[]{:S(2)}) collective-permute-start(bf16[512,768]{1,0:T(8,128)(2,1)S(1)} %shard_map.126.refs_1_.refs_0_), channel_id=1, source_target_pairs={{0,1},{1,0},{2,3},{3,2},{4,5},{5,4},{6,7},{7,6},{8,9},{9,8},{10,11... | collective-permute-start | bytes 2359304 | tf_op jit(solution)/shard_map/ppermute | solution.py:613
  182.2 12.4 %collective-permute-start.33 = (bf16[64,896]{1,0:T(8,128)(2,1)S(1)}, bf16[64,896]{1,0:T(8,128)(2,1)S(1)}, u32[]{:S(2)}, u32[]{:S(2)}) collective-permute-start(bf16[64,896]{1,0:T(8,128)(2,1)S(1)} %get-tuple-element.66), channel_id=1, source_target_pairs={{0,0},{8,1},{16,2},{24,3},{1,4},{9,5},{17,6},{25,7},{2,8},{10,9},{... | collective-permute-start | bytes 344072 | tf_op jit(solution)/shard_map/ppermute | solution.py:628
  182.9 16.7 %collective-permute-start.34 = (bf16[64,896]{1,0:T(8,128)(2,1)S(1)}, bf16[64,896]{1,0:T(8,128)(2,1)S(1)}, u32[]{:S(2)}, u32[]{:S(2)}) collective-permute-start(bf16[64,896]{1,0:T(8,128)(2,1)S(1)} %get-tuple-element.67), channel_id=1, source_target_pairs={{8,0},{0,1},{24,2},{16,3},{9,4},{1,5},{25,6},{17,7},{10,8},{2,9},{... | collective-permute-start | bytes 344072 | tf_op jit(solution)/shard_map/ppermute | solution.py:628
  185.7 15.8 %collective-permute-start.35 = (bf16[64,896]{1,0:T(8,128)(2,1)S(1)}, bf16[64,896]{1,0:T(8,128)(2,1)S(1)}, u32[]{:S(2)}, u32[]{:S(2)}) collective-permute-start(bf16[64,896]{1,0:T(8,128)(2,1)S(1)} %get-tuple-element.68), channel_id=1, source_target_pairs={{16,0},{24,1},{0,2},{8,3},{17,4},{25,5},{1,6},{9,7},{18,8},{26,9},... | collective-permute-start | bytes 344072 | tf_op jit(solution)/shard_map/ppermute | solution.py:628
  188.4 21.2 %collective-permute-start.36 = (bf16[64,896]{1,0:T(8,128)(2,1)S(1)}, bf16[64,896]{1,0:T(8,128)(2,1)S(1)}, u32[]{:S(2)}, u32[]{:S(2)}) collective-permute-start(bf16[64,896]{1,0:T(8,128)(2,1)S(1)} %get-tuple-element.69), channel_id=1, source_target_pairs={{24,0},{16,1},{8,2},{0,3},{25,4},{17,5},{9,6},{1,7},{26,8},{18,9},... | collective-permute-start | bytes 344072 | tf_op jit(solution)/shard_map/ppermute | solution.py:628
  193.1 16.5 %collective-permute-start.37 = (bf16[64,896]{1,0:T(8,128)(2,1)S(1)}, bf16[64,896]{1,0:T(8,128)(2,1)S(1)}, u32[]{:S(2)}, u32[]{:S(2)}) collective-permute-start(bf16[64,896]{1,0:T(8,128)(2,1)S(1)} %get-tuple-element.70), channel_id=1, source_target_pairs={{1,0},{9,1},{17,2},{25,3},{0,4},{8,5},{16,6},{24,7},{3,8},{11,9},{... | collective-permute-start | bytes 344072 | tf_op jit(solution)/shard_map/ppermute | solution.py:628
  194.6 15.1 %collective-permute-start.38 = (bf16[64,896]{1,0:T(8,128)(2,1)S(1)}, bf16[64,896]{1,0:T(8,128)(2,1)S(1)}, u32[]{:S(2)}, u32[]{:S(2)}) collective-permute-start(bf16[64,896]{1,0:T(8,128)(2,1)S(1)} %get-tuple-element.71), channel_id=1, source_target_pairs={{9,0},{1,1},{25,2},{17,3},{8,4},{0,5},{24,6},{16,7},{11,8},{3,9},{... | collective-permute-start | bytes 344072 | tf_op jit(solution)/shard_map/ppermute | solution.py:628
  199.6 10.1 %collective-permute-start.39 = (bf16[64,896]{1,0:T(8,128)(2,1)S(1)}, bf16[64,896]{1,0:T(8,128)(2,1)S(1)}, u32[]{:S(2)}, u32[]{:S(2)}) collective-permute-start(bf16[64,896]{1,0:T(8,128)(2,1)S(1)} %get-tuple-element.72), channel_id=1, source_target_pairs={{17,0},{25,1},{1,2},{9,3},{16,4},{24,5},{0,6},{8,7},{19,8},{27,9},... | collective-permute-start | bytes 344072 | tf_op jit(solution)/shard_map/ppermute | solution.py:628
  (29 other events, 184.7 us)

commit v2 on v1

--- a/solution.py
+++ b/solution.py
@@ -598,7 +598,7 @@
             send = recv[s - 1][part] if s else None
             if s < first_back:
                 send = hop(place, s, count, chips, send, sums[s % count], part)
-            elif s > first_back and part == 0:
+            elif s > first_back and (part == 0 or s == slots - 1):
                 k = len(mine)
                 mine += pick(place, k, 1)
                 grads, token = gradients(
@@ -608,14 +608,12 @@
             came.append(lax.ppermute(send, "dp", ring))
         recv.append(came)
 
-    ready = len(mine)
-    mine += pick(place, ready, early - ready)
+    assert len(mine) == early
     others = [lax.ppermute(message, "dp", swap) for message in mine]
     acc, token = sum_rows(scalars, 0, mine, gate_and_up, None, 0)
     last = pick(token, early, count - early)
-    mine += last
     others += [lax.ppermute(message, "dp", swap) for message in last]
-    grads, token = gradients(token, ready, count, inv_root, x_t, g, mine[ready:], grads)
+    grads, token = gradients(token, early, count, inv_root, x_t, g, last, grads)
     units = [*last, *others]
     pieces = sum_rows(token, early, units, gate_and_up, acc, groups)
     returned = []

time: 216 us -> 221 us (1.023)
  waiting for transfers between devices: 63.4 us -> 68.5 us
    ppermute x20, waiting for transfers between devices: 24.6 us -> 29.1 us  [body(): came.append(lax.ppermute(send, 'dp', ring))]
    pallas_call x4 -> x5, Pallas kernels: 13.8 us -> 14.9 us  [gradients(): pl.pallas_call(functools.partial(gradients_kernel, units, scale, grads is...]
  transfers between devices with their start and end apart: 43 -> 43, of which waited for: 24 -> 25; matrix products, arithmetic and copies ran while one was open for 0% -> 0% of each run, Pallas kernels for 22% -> 21%
where the time goes in v2:
time: 221 us; the launch traced here: 218 us
  starting transfers between devices  81.1 us (37%)
  waiting for transfers between devices  68.5 us (31%)
  Pallas kernels  65.2 us (30%)
    ppermute x20, starting transfers between devices, body(): came.append(lax.ppermute(send, 'dp', ring))  41 us
    ppermute x20, waiting for transfers between devices, body(): came.append(lax.ppermute(send, 'dp', ring))  29.1 us
    ppermute x8, starting transfers between devices, body(): returned.append(lax.ppermute(piece, ('expert', 'dp'), pairs))  21.7 us
    ppermute x6, waiting for transfers between devices, exchange(): lax.ppermute(messages[t], 'expert', [(q, q ^ t) for q in range(experts)])  20.8 us
    all_to_all x2, waiting for transfers between devices, exchange(): lax.all_to_all(blocks, 'dp', split_axis=0, concat_axis=0, tiled=True)  16.1 us
    pallas_call x5, Pallas kernels, gradients(): pl.pallas_call(functools.partial(gradients_kernel, units, scale, grads is...  14.9 us
    pallas_call x4, Pallas kernels, back_rows(): pl.pallas_call(back_kernel, out_shape=jax.ShapeDtypeStruct((size, slots,...  11.3 us
    pallas_call x1, Pallas kernels, gate_up(): pl.pallas_call(gate_up_kernel, out_shape=(out, out, jax.ShapeDtypeStruct(...  10.7 us
  transfers between devices with their start and end apart: 43, of which 25 were waited for; matrix products, arithmetic and copies ran while one was open for 0% of the time, Pallas kernels for 21%

profile of v2, /device:TPU:0, one launch (start us, length us, event | category | flops | bytes accessed | tf_op | source)
XLA Modules:
  0.0 218.4 jit_solution(7932948345305897321)
XLA Ops:
  3.4 3.0 %collective-permute-start.4 = (bf16[2,64,896]{2,1,0:T(8,128)(2,1)S(1)}, bf16[2,64,896]{2,1,0:T(8,128)(2,1)S(1)}, u32[]{:S(2)}, u32[]{:S(2)}) collective-permute-start(bf16[2,64,896]{2,1,0:T(8,128)(2,1)S(1)} %get-tuple-element.53), channel_id=1, source_target_pairs={{0,8},{8,0},{16,24},{24,16},{1,9},{9,1},{17,25},{25,17},{2,10},{10... | collective-permute-start | bytes 688136 | tf_op jit(solution)/shard_map/ppermute | solution.py:560
  8.0 4.9 %collective-permute-done.4.refs_1_ = bf16[2,64,896]{2,1,0:T(8,128)(2,1)S(1)} collective-permute-done((bf16[2,64,896]{2,1,0:T(8,128)(2,1)S(1)}, bf16[2,64,896]{2,1,0:T(8,128)(2,1)S(1)}, u32[]{:S(2)}, u32[]{:S(2)}) %collective-permute-start.4) | collective-permute-done | bytes 229408 | tf_op jit(solution)/shard_map/ppermute | solution.py:560
  12.9 5.5 %collective-permute-done.5.refs_2_ = bf16[2,64,896]{2,1,0:T(8,128)(2,1)S(1)} collective-permute-done((bf16[2,64,896]{2,1,0:T(8,128)(2,1)S(1)}, bf16[2,64,896]{2,1,0:T(8,128)(2,1)S(1)}, u32[]{:S(2)}, u32[]{:S(2)}) %collective-permute-start.5) | collective-permute-done | bytes 229408 | tf_op jit(solution)/shard_map/ppermute | solution.py:560
  18.4 2.7 %shard_map.106 = bf16[4,2,64,896]{3,2,1,0:T(8,128)(2,1)} custom-call(s32[21]{0:T(128)S(1)} %stack.87.scalar_ref, bf16[2,64,896]{2,1,0:T(8,128)(2,1)S(1)} %get-tuple-element.52.refs_0_, bf16[2,64,896]{2,1,0:T(8,128)(2,1)S(1)} %collective-permute-done.4.refs_1_, bf16[2,64,896]{2,1,0:T(8,128)(2,1)S(1)} %collective-permute-done.5.refs_2_, ...), custom_call_target="tpu_custom_call" | custom-call | flops 1024 | bytes 1024 | tf_op jit(solution)/shard_map/pallas_call | solution.py:131
  21.1 4.9 %all-to-all-start.1 = ((bf16[8,64,896]{2,1,0:T(8,128)(2,1)}), bf16[8,64,896]{2,1,0:T(8,128)(2,1)S(1)}, u32[]{:S(2)}, u32[]{:S(2)}) async-start(bf16[8,64,896]{2,1,0:T(8,128)(2,1)} %bitcast.26), calls=%async_computation.1 | async-start | bytes 1835008 | tf_op jit(solution)/shard_map/all_to_all | solution.py:562
  31.9 4.9 %collective-permute-done.refs_1_ = bf16[2,64,896]{2,1,0:T(8,128)(2,1)S(1)} collective-permute-done((bf16[2,64,896]{2,1,0:T(8,128)(2,1)S(1)}, bf16[2,64,896]{2,1,0:T(8,128)(2,1)S(1)}, u32[]{:S(2)}, u32[]{:S(2)}) %collective-permute-start) | collective-permute-done | bytes 229408 | tf_op jit(solution)/shard_map/ppermute | solution.py:560
  36.9 3.9 %collective-permute-done.1.refs_2_ = bf16[2,64,896]{2,1,0:T(8,128)(2,1)S(1)} collective-permute-done((bf16[2,64,896]{2,1,0:T(8,128)(2,1)S(1)}, bf16[2,64,896]{2,1,0:T(8,128)(2,1)S(1)}, u32[]{:S(2)}, u32[]{:S(2)}) %collective-permute-start.1) | collective-permute-done | bytes 229408 | tf_op jit(solution)/shard_map/ppermute | solution.py:560
  42.3 2.7 %shard_map.104 = bf16[4,2,64,896]{3,2,1,0:T(8,128)(2,1)} custom-call(s32[21]{0:T(128)S(1)} %stack.87.scalar_ref, bf16[2,64,896]{2,1,0:T(8,128)(2,1)S(1)} %get-tuple-element.48.refs_0_, bf16[2,64,896]{2,1,0:T(8,128)(2,1)S(1)} %collective-permute-done.refs_1_, bf16[2,64,896]{2,1,0:T(8,128)(2,1)S(1)} %collective-permute-done.1.refs_2_, ...), custom_call_target="tpu_custom_call" | custom-call | flops 1024 | bytes 1024 | tf_op jit(solution)/shard_map/pallas_call | solution.py:131
  45.0 4.8 %all-to-all-done.1 = bf16[8,64,896]{2,1,0:T(8,128)(2,1)S(1)} async-done(((bf16[8,64,896]{2,1,0:T(8,128)(2,1)}), bf16[8,64,896]{2,1,0:T(8,128)(2,1)S(1)}, u32[]{:S(2)}, u32[]{:S(2)}) %all-to-all-start.1) | async-done | bytes 917536 | tf_op jit(solution)/shard_map/all_to_all | solution.py:562
  49.8 3.6 %all-to-all-start = ((bf16[8,64,896]{2,1,0:T(8,128)(2,1)}), bf16[8,64,896]{2,1,0:T(8,128)(2,1)S(1)}, u32[]{:S(2)}, u32[]{:S(2)}) async-start(bf16[8,64,896]{2,1,0:T(8,128)(2,1)} %bitcast.23), calls=%async_computation | async-start | bytes 1835008 | tf_op jit(solution)/shard_map/all_to_all | solution.py:562
  53.4 10.7 %shard_map.107 = (bf16[4,512,512]{2,1,0:T(8,128)(2,1)}, bf16[4,512,512]{2,1,0:T(8,128)(2,1)S(1)}, bf16[896,512]{1,0:T(8,128)(2,1)S(1)}) custom-call(s32[21]{0:T(128)S(1)} %stack.87.scalar_ref, bf16[512,896]{1,0:T(8,128)(2,1)S(1)} %bitcast.42, bf16[896,2048]{1,0:T(8,128)(2,1)} %bitcast.43, bf16[896,2048]{1,0:T(8,128)(2,1)} %bitcast.52), custom_call_target="tpu_custom_call" | custom-call | flops 1024 | bytes 1024 | tf_op jit(solution)/shard_map/pallas_call | solution.py:229
  65.8 11.3 %all-to-all-done = bf16[8,64,896]{2,1,0:T(8,128)(2,1)S(1)} async-done(((bf16[8,64,896]{2,1,0:T(8,128)(2,1)}), bf16[8,64,896]{2,1,0:T(8,128)(2,1)S(1)}, u32[]{:S(2)}, u32[]{:S(2)}) %all-to-all-start) | async-done | bytes 917536 | tf_op jit(solution)/shard_map/all_to_all | solution.py:562
  77.1 2.6 %shard_map.105 = bf16[2,512,256]{2,1,0:T(8,128)(2,1)S(1)} custom-call(s32[21]{0:T(128)S(1)} %stack.87.scalar_ref, bf16[512,896]{1,0:T(8,128)(2,1)S(1)} %bitcast.33, bf16[2048,896]{1,0:T(8,128)(2,1)} %bitcast.61), custom_call_target="tpu_custom_call" | custom-call | flops 1024 | bytes 1024 | tf_op jit(solution)/shard_map/pallas_call | solution.py:272
  81.7 3.1 %shard_map.108.refs_0_.refs_1_ = bf16[2,512,768]{2,1,0:T(8,128)(2,1)S(1)} custom-call(s32[21]{0:T(128)S(1)} %stack.87.scalar_ref, bf16[512,896]{1,0:T(8,128)(2,1)S(1)} %bitcast.34, bf16[2048,896]{1,0:T(8,128)(2,1)} %bitcast.62, bf16[2,512,256]{2,1,0:T(8,128)(2,1)S(1)} %collective-permute-done.3.refs_0_, bf16[4,512,512]{2,1,0:T(8,128)(2,1)S(1)} %copy-done.1, ...), custom_call_target="tpu_custom_call" | custom-call | flops 1024 | bytes 1024 | tf_op jit(solution)/shard_map/pallas_call | solution.py:272
  97.0 3.1 %shard_map.112.refs_1_ = bf16[2,512,768]{2,1,0:T(8,128)(2,1)S(1)} custom-call(s32[21]{0:T(128)S(1)} %stack.87.scalar_ref, bf16[512,896]{1,0:T(8,128)(2,1)S(1)} %bitcast.36, bf16[2048,896]{1,0:T(8,128)(2,1)} %bitcast.64, bf16[2,512,256]{2,1,0:T(8,128)(2,1)S(1)} %collective-permute-done.10.refs_0_, bf16[4,512,512]{2,1,0:T(8,128)(2,1)S(1)} %copy-done.1, ...), custom_call_target="tpu_custom_call" | custom-call | flops 1024 | bytes 1024 | tf_op jit(solution)/shard_map/pallas_call | solution.py:272
  158.6 3.2 %collective-permute-done.26.refs_7_.in_ref.refs_5_ = bf16[256,768]{1,0:T(8,128)(2,1)S(1)} collective-permute-done((bf16[256,768]{1,0:T(8,128)(2,1)S(1)}, bf16[256,768]{1,0:T(8,128)(2,1)S(1)}, u32[]{:S(2)}, u32[]{:S(2)}) %collective-permute-start.26) | collective-permute-done | bytes 393248 | tf_op jit(solution)/shard_map/ppermute | solution.py:608
  169.6 4.2 %shard_map.130 = (f32[512,896]{1,0:T(8,128)S(1)}, s32[21]{0:T(128)S(1)}) custom-call(s32[21]{0:T(128)S(1)} %stack.87.scalar_ref, bf16[512,768]{1,0:T(8,128)(2,1)S(1)} %shard_map.125.refs_0_, bf16[512,768]{1,0:T(8,128)(2,1)S(1)} %shard_map.126.refs_1_.refs_0_, bf16[512,768]{1,0:T(8,128)(2,1)S(1)} %shard_map.129.refs_2_.refs_0_, bf16[896,2048]{1,0:T(8,128)(2,1)} %bitcast.44, ...), custom_call_target="tpu_custom_call" | custom-call | flops 1024 | bytes 1024 | tf_op jit(solution)/shard_map/pallas_call | solution.py:514
  173.9 3.1 %collective-permute-done.27.refs_6_ = bf16[256,768]{1,0:T(8,128)(2,1)S(1)} collective-permute-done((bf16[256,768]{1,0:T(8,128)(2,1)S(1)}, bf16[256,768]{1,0:T(8,128)(2,1)S(1)}, u32[]{:S(2)}, u32[]{:S(2)}) %collective-permute-start.27) | collective-permute-done | bytes 393248 | tf_op jit(solution)/shard_map/ppermute | solution.py:608
  180.7 5.9 %shard_map.137 = (bf16[64,896]{1,0:T(8,128)(2,1)S(1)}, bf16[64,896]{1,0:T(8,128)(2,1)S(1)}, bf16[64,896]{1,0:T(8,128)(2,1)S(1)}, bf16[64,896]{1,0:T(8,128)(2,1)S...) custom-call(s32[21]{0:T(128)S(1)} %get-tuple-element.72.scalar_ref, ...), custom_call_target="tpu_custom_call" | custom-call | flops 1024 | bytes 1024 | tf_op jit(solution)/shard_map/pallas_call | solution.py:514
  187.3 4.0 %collective-permute-start.34 = (bf16[64,896]{1,0:T(8,128)(2,1)S(1)}, bf16[64,896]{1,0:T(8,128)(2,1)S(1)}, u32[]{:S(2)}, u32[]{:S(2)}) collective-permute-start(bf16[64,896]{1,0:T(8,128)(2,1)S(1)} %get-tuple-element.75), channel_id=1, source_target_pairs={{8,0},{0,1},{24,2},{16,3},{9,4},{1,5},{25,6},{17,7},{10,8},{2,9},{... | collective-permute-start | bytes 344072 | tf_op jit(solution)/shard_map/ppermute | solution.py:626
  194.0 4.7 %collective-permute-start.36 = (bf16[64,896]{1,0:T(8,128)(2,1)S(1)}, bf16[64,896]{1,0:T(8,128)(2,1)S(1)}, u32[]{:S(2)}, u32[]{:S(2)}) collective-permute-start(bf16[64,896]{1,0:T(8,128)(2,1)S(1)} %get-tuple-element.77), channel_id=1, source_target_pairs={{24,0},{16,1},{8,2},{0,3},{25,4},{17,5},{9,6},{1,7},{26,8},{18,9},... | collective-permute-start | bytes 344072 | tf_op jit(solution)/shard_map/ppermute | solution.py:626
  200.2 5.0 %collective-permute-start.38 = (bf16[64,896]{1,0:T(8,128)(2,1)S(1)}, bf16[64,896]{1,0:T(8,128)(2,1)S(1)}, u32[]{:S(2)}, u32[]{:S(2)}) collective-permute-start(bf16[64,896]{1,0:T(8,128)(2,1)S(1)} %get-tuple-element.79), channel_id=1, source_target_pairs={{9,0},{1,1},{25,2},{17,3},{8,4},{0,5},{24,6},{16,7},{11,8},{3,9},{... | collective-permute-start | bytes 344072 | tf_op jit(solution)/shard_map/ppermute | solution.py:626
  208.4 5.6 %shard_map.139 = (bf16[896,2048]{1,0:T(8,128)(2,1)}, bf16[896,2048]{1,0:T(8,128)(2,1)}, bf16[2048,896]{1,0:T(8,128)(2,1)}, s32[21]{0:T(128)}) custom-call(s32[21]{0:T(128)S(1)} %stack.87.scalar_ref, bf16[896,512]{1,0:T(8,128)(2,1)S(1)} %get-tuple-element.58.xt_ref, ...), custom_call_target="tpu_custom_call", output_to_operand_aliasing={{0}: (7, {}), {1}: (8, {}), {2}: (9, {})} | custom-call | flops 1024 | bytes 1024 | tf_op jit(solution)/shard_map/pallas_call | solution.py:446
  215.3 2.9 %shard_map.138 = bf16[128,1792]{1,0:T(8,128)(2,1)} custom-call(s32[21]{0:T(128)S(1)} %stack.87.scalar_ref, bf16[256,128]{1,0:T(8,128)(2,1)S(1)} %get-tuple-element.47.hot_ref, bf16[64,896]{1,0:T(8,128)(2,1)} %copy-done.2, bf16[64,896]{1,0:T(8,128)(2,1)} %copy-done.3, bf16[64,896]{1,0:T(8,128)(2,1)} %copy-done.4, bf16[64,896]{1,0:T(8,128)(2,1)} %copy-done.5, ...), custom_call_target="tpu_custom_call" | custom-call | flops 1024 | bytes 1024 | tf_op jit(solution)/shard_map/pallas_call | solution.py:184
  (121 shorter events, 106.6 us)
Async XLA Ops:
  3.4 9.4 %collective-permute-start.4 = (bf16[2,64,896]{2,1,0:T(8,128)(2,1)S(1)}, bf16[2,64,896]{2,1,0:T(8,128)(2,1)S(1)}, u32[]{:S(2)}, u32[]{:S(2)}) collective-permute-start(bf16[2,64,896]{2,1,0:T(8,128)(2,1)S(1)} %get-tuple-element.53), channel_id=1, source_target_pairs={{0,8},{8,0},{16,24},{24,16},{1,9},{9,1},{17,25},{25,17},{2,10},{10... | collective-permute-start | bytes 688136 | tf_op jit(solution)/shard_map/ppermute | solution.py:560
  6.4 12.0 %collective-permute-start.5 = (bf16[2,64,896]{2,1,0:T(8,128)(2,1)S(1)}, bf16[2,64,896]{2,1,0:T(8,128)(2,1)S(1)}, u32[]{:S(2)}, u32[]{:S(2)}) collective-permute-start(bf16[2,64,896]{2,1,0:T(8,128)(2,1)S(1)} %get-tuple-element.54), channel_id=1, source_target_pairs={{0,16},{8,24},{16,0},{24,8},{1,17},{9,25},{17,1},{25,9},{2,18},{10... | collective-permute-start | bytes 688136 | tf_op jit(solution)/shard_map/ppermute | solution.py:560
  7.9 10.5 %collective-permute-start.6 = (bf16[2,64,896]{2,1,0:T(8,128)(2,1)S(1)}, bf16[2,64,896]{2,1,0:T(8,128)(2,1)S(1)}, u32[]{:S(2)}, u32[]{:S(2)}) collective-permute-start(bf16[2,64,896]{2,1,0:T(8,128)(2,1)S(1)} %get-tuple-element.55), channel_id=1, source_target_pairs={{0,24},{8,16},{16,8},{24,0},{1,25},{9,17},{17,9},{25,1},{2,26},{10... | collective-permute-start | bytes 688136 | tf_op jit(solution)/shard_map/ppermute | solution.py:560
  21.1 28.7 %all-to-all-start.1 = ((bf16[8,64,896]{2,1,0:T(8,128)(2,1)}), bf16[8,64,896]{2,1,0:T(8,128)(2,1)S(1)}, u32[]{:S(2)}, u32[]{:S(2)}) async-start(bf16[8,64,896]{2,1,0:T(8,128)(2,1)} %bitcast.26), calls=%async_computation.1 | async-start | bytes 1835008 | tf_op jit(solution)/shard_map/all_to_all | solution.py:562
  28.4 8.5 %collective-permute-start = (bf16[2,64,896]{2,1,0:T(8,128)(2,1)S(1)}, bf16[2,64,896]{2,1,0:T(8,128)(2,1)S(1)}, u32[]{:S(2)}, u32[]{:S(2)}) collective-permute-start(bf16[2,64,896]{2,1,0:T(8,128)(2,1)S(1)} %get-tuple-element.49), channel_id=1, source_target_pairs={{0,8},{8,0},{16,24},{24,16},{1,9},{9,1},{17,25},{25,17},{2,10},{10... | collective-permute-start | bytes 688136 | tf_op jit(solution)/shard_map/ppermute | solution.py:560
  29.7 11.0 %collective-permute-start.1 = (bf16[2,64,896]{2,1,0:T(8,128)(2,1)S(1)}, bf16[2,64,896]{2,1,0:T(8,128)(2,1)S(1)}, u32[]{:S(2)}, u32[]{:S(2)}) collective-permute-start(bf16[2,64,896]{2,1,0:T(8,128)(2,1)S(1)} %get-tuple-element.50), channel_id=1, source_target_pairs={{0,16},{8,24},{16,0},{24,8},{1,17},{9,25},{17,1},{25,9},{2,18},{10... | collective-permute-start | bytes 688136 | tf_op jit(solution)/shard_map/ppermute | solution.py:560
  30.5 11.8 %collective-permute-start.2 = (bf16[2,64,896]{2,1,0:T(8,128)(2,1)S(1)}, bf16[2,64,896]{2,1,0:T(8,128)(2,1)S(1)}, u32[]{:S(2)}, u32[]{:S(2)}) collective-permute-start(bf16[2,64,896]{2,1,0:T(8,128)(2,1)S(1)} %get-tuple-element.51), channel_id=1, source_target_pairs={{0,24},{8,16},{16,8},{24,0},{1,25},{9,17},{17,9},{25,1},{2,26},{10... | collective-permute-start | bytes 688136 | tf_op jit(solution)/shard_map/ppermute | solution.py:560
  49.8 27.3 %all-to-all-start = ((bf16[8,64,896]{2,1,0:T(8,128)(2,1)}), bf16[8,64,896]{2,1,0:T(8,128)(2,1)S(1)}, u32[]{:S(2)}, u32[]{:S(2)}) async-start(bf16[8,64,896]{2,1,0:T(8,128)(2,1)} %bitcast.23), calls=%async_computation | async-start | bytes 1835008 | tf_op jit(solution)/shard_map/all_to_all | solution.py:562
  65.4 16.3 %collective-permute-start.7 = (bf16[4,512,512]{2,1,0:T(8,128)(2,1)}, bf16[4,512,512]{2,1,0:T(8,128)(2,1)}, u32[]{:S(2)}, u32[]{:S(2)}) collective-permute-start(bf16[4,512,512]{2,1,0:T(8,128)(2,1)} %get-tuple-element.57), channel_id=1, source_target_pairs={{0,1},{1,0},{2,3},{3,2},{4,5},{5,4},{6,7},{7,6},{8,9},{9,8},{10,11... | collective-permute-start | bytes 6291464 | tf_op jit(solution)/shard_map/ppermute | solution.py:571
  84.9 9.5 %collective-permute-start.13 = (bf16[256,768]{1,0:T(8,128)(2,1)S(1)}, bf16[256,768]{1,0:T(8,128)(2,1)S(1)}, u32[]{:S(2)}, u32[]{:S(2)}) collective-permute-start(bf16[256,768]{1,0:T(8,128)(2,1)S(1)} %shard_map.115), channel_id=1, source_target_pairs={{0,2},{2,4},{4,6},{6,7},{7,5},{5,3},{3,1},{1,0},{8,10},{10,12},{12... | collective-permute-start | bytes 1179656 | tf_op jit(solution)/shard_map/ppermute | solution.py:608
  87.6 9.4 %collective-permute-start.10 = (bf16[2,512,256]{2,1,0:T(8,128)(2,1)S(1)}, bf16[2,512,256]{2,1,0:T(8,128)(2,1)S(1)}, u32[]{:S(2)}, u32[]{:S(2)}) collective-permute-start(bf16[2,512,256]{2,1,0:T(8,128)(2,1)S(1)} %shard_map.111), channel_id=1, source_target_pairs={{0,1},{1,0},{2,3},{3,2},{4,5},{5,4},{6,7},{7,6},{8,9},{9,8},{10,11... | collective-permute-start | bytes 1572872 | tf_op jit(solution)/shard_map/ppermute | solution.py:574
  90.2 9.8 %collective-permute-start.9 = (bf16[256,768]{1,0:T(8,128)(2,1)S(1)}, bf16[256,768]{1,0:T(8,128)(2,1)S(1)}, u32[]{:S(2)}, u32[]{:S(2)}) collective-permute-start(bf16[256,768]{1,0:T(8,128)(2,1)S(1)} %shard_map.110), channel_id=1, source_target_pairs={{0,2},{2,4},{4,6},{6,7},{7,5},{5,3},{3,1},{1,0},{8,10},{10,12},{12... | collective-permute-start | bytes 1179656 | tf_op jit(solution)/shard_map/ppermute | solution.py:608
  140.7 9.6 %collective-permute-start.23 = (bf16[256,768]{1,0:T(8,128)(2,1)S(1)}, bf16[256,768]{1,0:T(8,128)(2,1)S(1)}, u32[]{:S(2)}, u32[]{:S(2)}) collective-permute-start(bf16[256,768]{1,0:T(8,128)(2,1)S(1)} %collective-permute-done.21.refs_6_.refs_4_.refs_2_.refs_0_), channel_id=1, source_target_pairs={{0,2},{2,4},{4,6},{6,7},{7,5},{5,3},{3,1},{1,0},{8,10},{10,12},{12... | collective-permute-start | bytes 1179656 | tf_op jit(solution)/shard_map/ppermute | solution.py:608
  165.1 8.9 %collective-permute-start.28 = (bf16[256,768]{1,0:T(8,128)(2,1)S(1)}, bf16[256,768]{1,0:T(8,128)(2,1)S(1)}, u32[]{:S(2)}, u32[]{:S(2)}) collective-permute-start(bf16[256,768]{1,0:T(8,128)(2,1)S(1)} %shard_map.134), channel_id=1, source_target_pairs={{0,2},{2,4},{4,6},{6,7},{7,5},{5,3},{3,1},{1,0},{8,10},{10,12},{12... | collective-permute-start | bytes 1179656 | tf_op jit(solution)/shard_map/ppermute | solution.py:608
  168.1 8.9 %collective-permute-start.27 = (bf16[256,768]{1,0:T(8,128)(2,1)S(1)}, bf16[256,768]{1,0:T(8,128)(2,1)S(1)}, u32[]{:S(2)}, u32[]{:S(2)}) collective-permute-start(bf16[256,768]{1,0:T(8,128)(2,1)S(1)} %shard_map.132), channel_id=1, source_target_pairs={{0,2},{2,4},{4,6},{6,7},{7,5},{5,3},{3,1},{1,0},{8,10},{10,12},{12... | collective-permute-start | bytes 1179656 | tf_op jit(solution)/shard_map/ppermute | solution.py:608
  169.1 11.6 %collective-permute-start.29 = (bf16[512,768]{1,0:T(8,128)(2,1)S(1)}, bf16[512,768]{1,0:T(8,128)(2,1)S(1)}, u32[]{:S(2)}, u32[]{:S(2)}) collective-permute-start(bf16[512,768]{1,0:T(8,128)(2,1)S(1)} %shard_map.125.refs_0_), channel_id=1, source_target_pairs={{0,1},{1,0},{2,3},{3,2},{4,5},{5,4},{6,7},{7,6},{8,9},{9,8},{10,11... | collective-permute-start | bytes 2359304 | tf_op jit(solution)/shard_map/ppermute | solution.py:612
  169.1 11.6 %collective-permute-start.30 = (bf16[512,768]{1,0:T(8,128)(2,1)S(1)}, bf16[512,768]{1,0:T(8,128)(2,1)S(1)}, u32[]{:S(2)}, u32[]{:S(2)}) collective-permute-start(bf16[512,768]{1,0:T(8,128)(2,1)S(1)} %shard_map.126.refs_1_.refs_0_), channel_id=1, source_target_pairs={{0,1},{1,0},{2,3},{3,2},{4,5},{5,4},{6,7},{7,6},{8,9},{9,8},{10,11... | collective-permute-start | bytes 2359304 | tf_op jit(solution)/shard_map/ppermute | solution.py:612
  186.7 13.5 %collective-permute-start.33 = (bf16[64,896]{1,0:T(8,128)(2,1)S(1)}, bf16[64,896]{1,0:T(8,128)(2,1)S(1)}, u32[]{:S(2)}, u32[]{:S(2)}) collective-permute-start(bf16[64,896]{1,0:T(8,128)(2,1)S(1)} %get-tuple-element.74), channel_id=1, source_target_pairs={{0,0},{8,1},{16,2},{24,3},{1,4},{9,5},{17,6},{25,7},{2,8},{10,9},{... | collective-permute-start | bytes 344072 | tf_op jit(solution)/shard_map/ppermute | solution.py:626
  187.3 17.9 %collective-permute-start.34 = (bf16[64,896]{1,0:T(8,128)(2,1)S(1)}, bf16[64,896]{1,0:T(8,128)(2,1)S(1)}, u32[]{:S(2)}, u32[]{:S(2)}) collective-permute-start(bf16[64,896]{1,0:T(8,128)(2,1)S(1)} %get-tuple-element.75), channel_id=1, source_target_pairs={{8,0},{0,1},{24,2},{16,3},{9,4},{1,5},{25,6},{17,7},{10,8},{2,9},{... | collective-permute-start | bytes 344072 | tf_op jit(solution)/shard_map/ppermute | solution.py:626
  191.4 15.8 %collective-permute-start.35 = (bf16[64,896]{1,0:T(8,128)(2,1)S(1)}, bf16[64,896]{1,0:T(8,128)(2,1)S(1)}, u32[]{:S(2)}, u32[]{:S(2)}) collective-permute-start(bf16[64,896]{1,0:T(8,128)(2,1)S(1)} %get-tuple-element.76), channel_id=1, source_target_pairs={{16,0},{24,1},{0,2},{8,3},{17,4},{25,5},{1,6},{9,7},{18,8},{26,9},... | collective-permute-start | bytes 344072 | tf_op jit(solution)/shard_map/ppermute | solution.py:626
  194.0 20.0 %collective-permute-start.36 = (bf16[64,896]{1,0:T(8,128)(2,1)S(1)}, bf16[64,896]{1,0:T(8,128)(2,1)S(1)}, u32[]{:S(2)}, u32[]{:S(2)}) collective-permute-start(bf16[64,896]{1,0:T(8,128)(2,1)S(1)} %get-tuple-element.77), channel_id=1, source_target_pairs={{24,0},{16,1},{8,2},{0,3},{25,4},{17,5},{9,6},{1,7},{26,8},{18,9},... | collective-permute-start | bytes 344072 | tf_op jit(solution)/shard_map/ppermute | solution.py:626
  198.8 15.3 %collective-permute-start.37 = (bf16[64,896]{1,0:T(8,128)(2,1)S(1)}, bf16[64,896]{1,0:T(8,128)(2,1)S(1)}, u32[]{:S(2)}, u32[]{:S(2)}) collective-permute-start(bf16[64,896]{1,0:T(8,128)(2,1)S(1)} %get-tuple-element.78), channel_id=1, source_target_pairs={{1,0},{9,1},{17,2},{25,3},{0,4},{8,5},{16,6},{24,7},{3,8},{11,9},{... | collective-permute-start | bytes 344072 | tf_op jit(solution)/shard_map/ppermute | solution.py:626
  200.2 13.9 %collective-permute-start.38 = (bf16[64,896]{1,0:T(8,128)(2,1)S(1)}, bf16[64,896]{1,0:T(8,128)(2,1)S(1)}, u32[]{:S(2)}, u32[]{:S(2)}) collective-permute-start(bf16[64,896]{1,0:T(8,128)(2,1)S(1)} %get-tuple-element.79), channel_id=1, source_target_pairs={{9,0},{1,1},{25,2},{17,3},{8,4},{0,5},{24,6},{16,7},{11,8},{3,9},{... | collective-permute-start | bytes 344072 | tf_op jit(solution)/shard_map/ppermute | solution.py:626
  205.2 8.9 %collective-permute-start.39 = (bf16[64,896]{1,0:T(8,128)(2,1)S(1)}, bf16[64,896]{1,0:T(8,128)(2,1)S(1)}, u32[]{:S(2)}, u32[]{:S(2)}) collective-permute-start(bf16[64,896]{1,0:T(8,128)(2,1)S(1)} %get-tuple-element.80), channel_id=1, source_target_pairs={{17,0},{25,1},{1,2},{9,3},{16,4},{24,5},{0,6},{8,7},{19,8},{27,9},... | collective-permute-start | bytes 344072 | tf_op jit(solution)/shard_map/ppermute | solution.py:626
  (29 other events, 178.2 us)

commit v3 on v1

--- a/solution.py
+++ b/solution.py
@@ -613,7 +613,6 @@
     others = [lax.ppermute(message, "dp", swap) for message in mine]
     acc, token = sum_rows(scalars, 0, mine, gate_and_up, None, 0)
     last = pick(token, early, count - early)
-    mine += last
     others += [lax.ppermute(message, "dp", swap) for message in last]
     grads, token = gradients(token, ready, count, inv_root, x_t, g, mine[ready:], grads)
     units = [*last, *others]
@@ -626,7 +625,7 @@
                 h, e = divmod(b ^ r, experts)
                 pairs.append((e * groups + 2 * q + h, q * groups + b))
         returned.append(lax.ppermute(piece, ("expert", "dp"), pairs))
-    grads, _ = gradients(scalars, count, count, inv_root, x_t, g, others, grads)
+    grads, _ = gradients(scalars, early, count, inv_root, x_t, g, units, grads)
     grad_tokens = combine_rows(scalars, hot, returned, experts)
     return (grad_tokens, grads[0][None], grads[1][None], grads[2][None])
 

time: 216 us -> 214 us (level)
  no operation moved by 1% of the time
where the time goes in v3:
time: 214 us; the launch traced here: 213 us
  starting transfers between devices  82.8 us (39%)
  waiting for transfers between devices  63.4 us (30%)
  Pallas kernels  63.3 us (30%)
  local copies, waits for them, and re-layouts  2.18 us (1%)
    ppermute x20, starting transfers between devices, body(): came.append(lax.ppermute(send, 'dp', ring))  41.5 us
    ppermute x20, waiting for transfers between devices, body(): came.append(lax.ppermute(send, 'dp', ring))  24.6 us
    ppermute x8, starting transfers between devices, body(): returned.append(lax.ppermute(piece, ('expert', 'dp'), pairs))  21.7 us
    ppermute x6, waiting for transfers between devices, exchange(): lax.ppermute(messages[t], 'expert', [(q, q ^ t) for q in range(experts)])  20.8 us
    all_to_all x2, waiting for transfers between devices, exchange(): lax.all_to_all(blocks, 'dp', split_axis=0, concat_axis=0, tiled=True)  16.1 us
    pallas_call x4, Pallas kernels, gradients(): pl.pallas_call(functools.partial(gradients_kernel, units, scale, grads is...  13.5 us
    pallas_call x4, Pallas kernels, back_rows(): pl.pallas_call(back_kernel, out_shape=jax.ShapeDtypeStruct((size, slots,...  11.3 us
    pallas_call x1, Pallas kernels, gate_up(): pl.pallas_call(gate_up_kernel, out_shape=(out, out, jax.ShapeDtypeStruct(...  10.7 us
  transfers between devices with their start and end apart: 43, of which 24 were waited for; matrix products, arithmetic and copies ran while one was open for 0% of the time, Pallas kernels for 22%

profile of v3, /device:TPU:0, one launch (start us, length us, event | category | flops | bytes accessed | tf_op | source)
XLA Modules:
  0.0 213.3 jit_solution(1709271763016722)
XLA Ops:
  3.4 3.0 %collective-permute-start.4 = (bf16[2,64,896]{2,1,0:T(8,128)(2,1)S(1)}, bf16[2,64,896]{2,1,0:T(8,128)(2,1)S(1)}, u32[]{:S(2)}, u32[]{:S(2)}) collective-permute-start(bf16[2,64,896]{2,1,0:T(8,128)(2,1)S(1)} %get-tuple-element.49), channel_id=1, source_target_pairs={{0,8},{8,0},{16,24},{24,16},{1,9},{9,1},{17,25},{25,17},{2,10},{10... | collective-permute-start | bytes 688136 | tf_op jit(solution)/shard_map/ppermute | solution.py:560
  8.0 4.9 %collective-permute-done.4.refs_1_ = bf16[2,64,896]{2,1,0:T(8,128)(2,1)S(1)} collective-permute-done((bf16[2,64,896]{2,1,0:T(8,128)(2,1)S(1)}, bf16[2,64,896]{2,1,0:T(8,128)(2,1)S(1)}, u32[]{:S(2)}, u32[]{:S(2)}) %collective-permute-start.4) | collective-permute-done | bytes 229408 | tf_op jit(solution)/shard_map/ppermute | solution.py:560
  12.9 5.5 %collective-permute-done.5.refs_2_ = bf16[2,64,896]{2,1,0:T(8,128)(2,1)S(1)} collective-permute-done((bf16[2,64,896]{2,1,0:T(8,128)(2,1)S(1)}, bf16[2,64,896]{2,1,0:T(8,128)(2,1)S(1)}, u32[]{:S(2)}, u32[]{:S(2)}) %collective-permute-start.5) | collective-permute-done | bytes 229408 | tf_op jit(solution)/shard_map/ppermute | solution.py:560
  18.4 2.7 %shard_map.106 = bf16[4,2,64,896]{3,2,1,0:T(8,128)(2,1)} custom-call(s32[21]{0:T(128)S(1)} %stack.87.scalar_ref, bf16[2,64,896]{2,1,0:T(8,128)(2,1)S(1)} %get-tuple-element.48.refs_0_, bf16[2,64,896]{2,1,0:T(8,128)(2,1)S(1)} %collective-permute-done.4.refs_1_, bf16[2,64,896]{2,1,0:T(8,128)(2,1)S(1)} %collective-permute-done.5.refs_2_, ...), custom_call_target="tpu_custom_call" | custom-call | flops 1024 | bytes 1024 | tf_op jit(solution)/shard_map/pallas_call | solution.py:131
  21.1 4.9 %all-to-all-start.1 = ((bf16[8,64,896]{2,1,0:T(8,128)(2,1)}), bf16[8,64,896]{2,1,0:T(8,128)(2,1)S(1)}, u32[]{:S(2)}, u32[]{:S(2)}) async-start(bf16[8,64,896]{2,1,0:T(8,128)(2,1)} %bitcast.26), calls=%async_computation.1 | async-start | bytes 1835008 | tf_op jit(solution)/shard_map/all_to_all | solution.py:562
  31.9 4.9 %collective-permute-done.refs_1_ = bf16[2,64,896]{2,1,0:T(8,128)(2,1)S(1)} collective-permute-done((bf16[2,64,896]{2,1,0:T(8,128)(2,1)S(1)}, bf16[2,64,896]{2,1,0:T(8,128)(2,1)S(1)}, u32[]{:S(2)}, u32[]{:S(2)}) %collective-permute-start) | collective-permute-done | bytes 229408 | tf_op jit(solution)/shard_map/ppermute | solution.py:560
  36.9 3.9 %collective-permute-done.1.refs_2_ = bf16[2,64,896]{2,1,0:T(8,128)(2,1)S(1)} collective-permute-done((bf16[2,64,896]{2,1,0:T(8,128)(2,1)S(1)}, bf16[2,64,896]{2,1,0:T(8,128)(2,1)S(1)}, u32[]{:S(2)}, u32[]{:S(2)}) %collective-permute-start.1) | collective-permute-done | bytes 229408 | tf_op jit(solution)/shard_map/ppermute | solution.py:560
  42.3 2.7 %shard_map.104 = bf16[4,2,64,896]{3,2,1,0:T(8,128)(2,1)} custom-call(s32[21]{0:T(128)S(1)} %stack.87.scalar_ref, bf16[2,64,896]{2,1,0:T(8,128)(2,1)S(1)} %get-tuple-element.44.refs_0_, bf16[2,64,896]{2,1,0:T(8,128)(2,1)S(1)} %collective-permute-done.refs_1_, bf16[2,64,896]{2,1,0:T(8,128)(2,1)S(1)} %collective-permute-done.1.refs_2_, ...), custom_call_target="tpu_custom_call" | custom-call | flops 1024 | bytes 1024 | tf_op jit(solution)/shard_map/pallas_call | solution.py:131
  45.0 4.8 %all-to-all-done.1 = bf16[8,64,896]{2,1,0:T(8,128)(2,1)S(1)} async-done(((bf16[8,64,896]{2,1,0:T(8,128)(2,1)}), bf16[8,64,896]{2,1,0:T(8,128)(2,1)S(1)}, u32[]{:S(2)}, u32[]{:S(2)}) %all-to-all-start.1) | async-done | bytes 917536 | tf_op jit(solution)/shard_map/all_to_all | solution.py:562
  49.8 3.6 %all-to-all-start = ((bf16[8,64,896]{2,1,0:T(8,128)(2,1)}), bf16[8,64,896]{2,1,0:T(8,128)(2,1)S(1)}, u32[]{:S(2)}, u32[]{:S(2)}) async-start(bf16[8,64,896]{2,1,0:T(8,128)(2,1)} %bitcast.23), calls=%async_computation | async-start | bytes 1835008 | tf_op jit(solution)/shard_map/all_to_all | solution.py:562
  53.4 10.7 %shard_map.107 = (bf16[4,512,512]{2,1,0:T(8,128)(2,1)}, bf16[4,512,512]{2,1,0:T(8,128)(2,1)S(1)}, bf16[896,512]{1,0:T(8,128)(2,1)S(1)}) custom-call(s32[21]{0:T(128)S(1)} %stack.87.scalar_ref, bf16[512,896]{1,0:T(8,128)(2,1)S(1)} %bitcast.41, bf16[896,2048]{1,0:T(8,128)(2,1)} %bitcast.42, bf16[896,2048]{1,0:T(8,128)(2,1)} %bitcast.51), custom_call_target="tpu_custom_call" | custom-call | flops 1024 | bytes 1024 | tf_op jit(solution)/shard_map/pallas_call | solution.py:229
  65.8 11.3 %all-to-all-done = bf16[8,64,896]{2,1,0:T(8,128)(2,1)S(1)} async-done(((bf16[8,64,896]{2,1,0:T(8,128)(2,1)}), bf16[8,64,896]{2,1,0:T(8,128)(2,1)S(1)}, u32[]{:S(2)}, u32[]{:S(2)}) %all-to-all-start) | async-done | bytes 917536 | tf_op jit(solution)/shard_map/all_to_all | solution.py:562
  77.1 2.6 %shard_map.105 = bf16[2,512,256]{2,1,0:T(8,128)(2,1)S(1)} custom-call(s32[21]{0:T(128)S(1)} %stack.87.scalar_ref, bf16[512,896]{1,0:T(8,128)(2,1)S(1)} %bitcast.33, bf16[2048,896]{1,0:T(8,128)(2,1)} %bitcast.60), custom_call_target="tpu_custom_call" | custom-call | flops 1024 | bytes 1024 | tf_op jit(solution)/shard_map/pallas_call | solution.py:272
  81.7 3.1 %shard_map.108.refs_0_.refs_1_ = bf16[2,512,768]{2,1,0:T(8,128)(2,1)S(1)} custom-call(s32[21]{0:T(128)S(1)} %stack.87.scalar_ref, bf16[512,896]{1,0:T(8,128)(2,1)S(1)} %bitcast.34, bf16[2048,896]{1,0:T(8,128)(2,1)} %bitcast.61, bf16[2,512,256]{2,1,0:T(8,128)(2,1)S(1)} %collective-permute-done.3.refs_0_, bf16[4,512,512]{2,1,0:T(8,128)(2,1)S(1)} %copy-done.1, ...), custom_call_target="tpu_custom_call" | custom-call | flops 1024 | bytes 1024 | tf_op jit(solution)/shard_map/pallas_call | solution.py:272
  97.0 3.1 %shard_map.112.refs_1_ = bf16[2,512,768]{2,1,0:T(8,128)(2,1)S(1)} custom-call(s32[21]{0:T(128)S(1)} %stack.87.scalar_ref, bf16[512,896]{1,0:T(8,128)(2,1)S(1)} %bitcast.36, bf16[2048,896]{1,0:T(8,128)(2,1)} %bitcast.63, bf16[2,512,256]{2,1,0:T(8,128)(2,1)S(1)} %collective-permute-done.10.refs_0_, bf16[4,512,512]{2,1,0:T(8,128)(2,1)S(1)} %copy-done.1, ...), custom_call_target="tpu_custom_call" | custom-call | flops 1024 | bytes 1024 | tf_op jit(solution)/shard_map/pallas_call | solution.py:272
  115.4 2.6 %collective-permute-start.17 = (bf16[256,768]{1,0:T(8,128)(2,1)S(1)}, bf16[256,768]{1,0:T(8,128)(2,1)S(1)}, u32[]{:S(2)}, u32[]{:S(2)}) collective-permute-start(bf16[256,768]{1,0:T(8,128)(2,1)S(1)} %shard_map.119), channel_id=1, source_target_pairs={{0,2},{2,4},{4,6},{6,7},{7,5},{5,3},{3,1},{1,0},{8,10},{10,12},{12... | collective-permute-start | bytes 1179656 | tf_op jit(solution)/shard_map/ppermute | solution.py:608
  165.2 4.2 %shard_map.130 = (f32[512,896]{1,0:T(8,128)S(1)}, s32[21]{0:T(128)S(1)}) custom-call(s32[21]{0:T(128)S(1)} %stack.87.scalar_ref, bf16[512,768]{1,0:T(8,128)(2,1)S(1)} %shard_map.125.refs_0_, bf16[512,768]{1,0:T(8,128)(2,1)S(1)} %shard_map.126.refs_1_.refs_0_, bf16[512,768]{1,0:T(8,128)(2,1)S(1)} %shard_map.129.refs_2_.refs_0_, bf16[896,2048]{1,0:T(8,128)(2,1)} %bitcast.43, ...), custom_call_target="tpu_custom_call" | custom-call | flops 1024 | bytes 1024 | tf_op jit(solution)/shard_map/pallas_call | solution.py:514
  175.0 5.9 %shard_map.135 = (bf16[64,896]{1,0:T(8,128)(2,1)S(1)}, bf16[64,896]{1,0:T(8,128)(2,1)S(1)}, bf16[64,896]{1,0:T(8,128)(2,1)S(1)}, bf16[64,896]{1,0:T(8,128)(2,1)S...) custom-call(s32[21]{0:T(128)S(1)} %get-tuple-element.63.scalar_ref, ...), custom_call_target="tpu_custom_call" | custom-call | flops 1024 | bytes 1024 | tf_op jit(solution)/shard_map/pallas_call | solution.py:514
  181.6 2.9 %collective-permute-start.34 = (bf16[64,896]{1,0:T(8,128)(2,1)S(1)}, bf16[64,896]{1,0:T(8,128)(2,1)S(1)}, u32[]{:S(2)}, u32[]{:S(2)}) collective-permute-start(bf16[64,896]{1,0:T(8,128)(2,1)S(1)} %get-tuple-element.67), channel_id=1, source_target_pairs={{8,0},{0,1},{24,2},{16,3},{9,4},{1,5},{25,6},{17,7},{10,8},{2,9},{... | collective-permute-start | bytes 344072 | tf_op jit(solution)/shard_map/ppermute | solution.py:627
  184.5 2.6 %collective-permute-start.35 = (bf16[64,896]{1,0:T(8,128)(2,1)S(1)}, bf16[64,896]{1,0:T(8,128)(2,1)S(1)}, u32[]{:S(2)}, u32[]{:S(2)}) collective-permute-start(bf16[64,896]{1,0:T(8,128)(2,1)S(1)} %get-tuple-element.68), channel_id=1, source_target_pairs={{16,0},{24,1},{0,2},{8,3},{17,4},{25,5},{1,6},{9,7},{18,8},{26,9},... | collective-permute-start | bytes 344072 | tf_op jit(solution)/shard_map/ppermute | solution.py:627
  187.1 4.7 %collective-permute-start.36 = (bf16[64,896]{1,0:T(8,128)(2,1)S(1)}, bf16[64,896]{1,0:T(8,128)(2,1)S(1)}, u32[]{:S(2)}, u32[]{:S(2)}) collective-permute-start(bf16[64,896]{1,0:T(8,128)(2,1)S(1)} %get-tuple-element.69), channel_id=1, source_target_pairs={{24,0},{16,1},{8,2},{0,3},{25,4},{17,5},{9,6},{1,7},{26,8},{18,9},... | collective-permute-start | bytes 344072 | tf_op jit(solution)/shard_map/ppermute | solution.py:627
  193.3 5.0 %collective-permute-start.38 = (bf16[64,896]{1,0:T(8,128)(2,1)S(1)}, bf16[64,896]{1,0:T(8,128)(2,1)S(1)}, u32[]{:S(2)}, u32[]{:S(2)}) collective-permute-start(bf16[64,896]{1,0:T(8,128)(2,1)S(1)} %get-tuple-element.71), channel_id=1, source_target_pairs={{9,0},{1,1},{25,2},{17,3},{8,4},{0,5},{24,6},{16,7},{11,8},{3,9},{... | collective-permute-start | bytes 344072 | tf_op jit(solution)/shard_map/ppermute | solution.py:627
  202.7 6.6 %shard_map.137 = (bf16[896,2048]{1,0:T(8,128)(2,1)}, bf16[896,2048]{1,0:T(8,128)(2,1)}, bf16[2048,896]{1,0:T(8,128)(2,1)}, s32[21]{0:T(128)}) custom-call(s32[21]{0:T(128)S(1)} %stack.87.scalar_ref, bf16[896,512]{1,0:T(8,128)(2,1)S(1)} %get-tuple-element.54.xt_ref, ...), custom_call_target="tpu_custom_call", output_to_operand_aliasing={{0}: (8, {}), {1}: (9, {}), {2}: (10, {})} | custom-call | flops 1024 | bytes 1024 | tf_op jit(solution)/shard_map/pallas_call | solution.py:446
  210.2 2.9 %shard_map.136 = bf16[128,1792]{1,0:T(8,128)(2,1)} custom-call(s32[21]{0:T(128)S(1)} %stack.87.scalar_ref, bf16[256,128]{1,0:T(8,128)(2,1)S(1)} %get-tuple-element.43.hot_ref, bf16[64,896]{1,0:T(8,128)(2,1)} %copy-done.2, bf16[64,896]{1,0:T(8,128)(2,1)} %copy-done.3, bf16[64,896]{1,0:T(8,128)(2,1)} %copy-done.4, bf16[64,896]{1,0:T(8,128)(2,1)} %copy-done.5, ...), custom_call_target="tpu_custom_call" | custom-call | flops 1024 | bytes 1024 | tf_op jit(solution)/shard_map/pallas_call | solution.py:184
  (119 shorter events, 102.7 us)
Async XLA Ops:
  3.4 9.4 %collective-permute-start.4 = (bf16[2,64,896]{2,1,0:T(8,128)(2,1)S(1)}, bf16[2,64,896]{2,1,0:T(8,128)(2,1)S(1)}, u32[]{:S(2)}, u32[]{:S(2)}) collective-permute-start(bf16[2,64,896]{2,1,0:T(8,128)(2,1)S(1)} %get-tuple-element.49), channel_id=1, source_target_pairs={{0,8},{8,0},{16,24},{24,16},{1,9},{9,1},{17,25},{25,17},{2,10},{10... | collective-permute-start | bytes 688136 | tf_op jit(solution)/shard_map/ppermute | solution.py:560
  6.4 12.0 %collective-permute-start.5 = (bf16[2,64,896]{2,1,0:T(8,128)(2,1)S(1)}, bf16[2,64,896]{2,1,0:T(8,128)(2,1)S(1)}, u32[]{:S(2)}, u32[]{:S(2)}) collective-permute-start(bf16[2,64,896]{2,1,0:T(8,128)(2,1)S(1)} %get-tuple-element.50), channel_id=1, source_target_pairs={{0,16},{8,24},{16,0},{24,8},{1,17},{9,25},{17,1},{25,9},{2,18},{10... | collective-permute-start | bytes 688136 | tf_op jit(solution)/shard_map/ppermute | solution.py:560
  7.9 10.5 %collective-permute-start.6 = (bf16[2,64,896]{2,1,0:T(8,128)(2,1)S(1)}, bf16[2,64,896]{2,1,0:T(8,128)(2,1)S(1)}, u32[]{:S(2)}, u32[]{:S(2)}) collective-permute-start(bf16[2,64,896]{2,1,0:T(8,128)(2,1)S(1)} %get-tuple-element.51), channel_id=1, source_target_pairs={{0,24},{8,16},{16,8},{24,0},{1,25},{9,17},{17,9},{25,1},{2,26},{10... | collective-permute-start | bytes 688136 | tf_op jit(solution)/shard_map/ppermute | solution.py:560
  21.1 28.7 %all-to-all-start.1 = ((bf16[8,64,896]{2,1,0:T(8,128)(2,1)}), bf16[8,64,896]{2,1,0:T(8,128)(2,1)S(1)}, u32[]{:S(2)}, u32[]{:S(2)}) async-start(bf16[8,64,896]{2,1,0:T(8,128)(2,1)} %bitcast.26), calls=%async_computation.1 | async-start | bytes 1835008 | tf_op jit(solution)/shard_map/all_to_all | solution.py:562
  28.4 8.5 %collective-permute-start = (bf16[2,64,896]{2,1,0:T(8,128)(2,1)S(1)}, bf16[2,64,896]{2,1,0:T(8,128)(2,1)S(1)}, u32[]{:S(2)}, u32[]{:S(2)}) collective-permute-start(bf16[2,64,896]{2,1,0:T(8,128)(2,1)S(1)} %get-tuple-element.45), channel_id=1, source_target_pairs={{0,8},{8,0},{16,24},{24,16},{1,9},{9,1},{17,25},{25,17},{2,10},{10... | collective-permute-start | bytes 688136 | tf_op jit(solution)/shard_map/ppermute | solution.py:560
  29.7 11.0 %collective-permute-start.1 = (bf16[2,64,896]{2,1,0:T(8,128)(2,1)S(1)}, bf16[2,64,896]{2,1,0:T(8,128)(2,1)S(1)}, u32[]{:S(2)}, u32[]{:S(2)}) collective-permute-start(bf16[2,64,896]{2,1,0:T(8,128)(2,1)S(1)} %get-tuple-element.46), channel_id=1, source_target_pairs={{0,16},{8,24},{16,0},{24,8},{1,17},{9,25},{17,1},{25,9},{2,18},{10... | collective-permute-start | bytes 688136 | tf_op jit(solution)/shard_map/ppermute | solution.py:560
  30.5 11.8 %collective-permute-start.2 = (bf16[2,64,896]{2,1,0:T(8,128)(2,1)S(1)}, bf16[2,64,896]{2,1,0:T(8,128)(2,1)S(1)}, u32[]{:S(2)}, u32[]{:S(2)}) collective-permute-start(bf16[2,64,896]{2,1,0:T(8,128)(2,1)S(1)} %get-tuple-element.47), channel_id=1, source_target_pairs={{0,24},{8,16},{16,8},{24,0},{1,25},{9,17},{17,9},{25,1},{2,26},{10... | collective-permute-start | bytes 688136 | tf_op jit(solution)/shard_map/ppermute | solution.py:560
  49.8 27.3 %all-to-all-start = ((bf16[8,64,896]{2,1,0:T(8,128)(2,1)}), bf16[8,64,896]{2,1,0:T(8,128)(2,1)S(1)}, u32[]{:S(2)}, u32[]{:S(2)}) async-start(bf16[8,64,896]{2,1,0:T(8,128)(2,1)} %bitcast.23), calls=%async_computation | async-start | bytes 1835008 | tf_op jit(solution)/shard_map/all_to_all | solution.py:562
  65.4 16.3 %collective-permute-start.7 = (bf16[4,512,512]{2,1,0:T(8,128)(2,1)}, bf16[4,512,512]{2,1,0:T(8,128)(2,1)}, u32[]{:S(2)}, u32[]{:S(2)}) collective-permute-start(bf16[4,512,512]{2,1,0:T(8,128)(2,1)} %get-tuple-element.53), channel_id=1, source_target_pairs={{0,1},{1,0},{2,3},{3,2},{4,5},{5,4},{6,7},{7,6},{8,9},{9,8},{10,11... | collective-permute-start | bytes 6291464 | tf_op jit(solution)/shard_map/ppermute | solution.py:571
  84.9 9.5 %collective-permute-start.13 = (bf16[256,768]{1,0:T(8,128)(2,1)S(1)}, bf16[256,768]{1,0:T(8,128)(2,1)S(1)}, u32[]{:S(2)}, u32[]{:S(2)}) collective-permute-start(bf16[256,768]{1,0:T(8,128)(2,1)S(1)} %shard_map.115), channel_id=1, source_target_pairs={{0,2},{2,4},{4,6},{6,7},{7,5},{5,3},{3,1},{1,0},{8,10},{10,12},{12... | collective-permute-start | bytes 1179656 | tf_op jit(solution)/shard_map/ppermute | solution.py:608
  87.6 9.4 %collective-permute-start.10 = (bf16[2,512,256]{2,1,0:T(8,128)(2,1)S(1)}, bf16[2,512,256]{2,1,0:T(8,128)(2,1)S(1)}, u32[]{:S(2)}, u32[]{:S(2)}) collective-permute-start(bf16[2,512,256]{2,1,0:T(8,128)(2,1)S(1)} %shard_map.111), channel_id=1, source_target_pairs={{0,1},{1,0},{2,3},{3,2},{4,5},{5,4},{6,7},{7,6},{8,9},{9,8},{10,11... | collective-permute-start | bytes 1572872 | tf_op jit(solution)/shard_map/ppermute | solution.py:574
  90.2 9.8 %collective-permute-start.9 = (bf16[256,768]{1,0:T(8,128)(2,1)S(1)}, bf16[256,768]{1,0:T(8,128)(2,1)S(1)}, u32[]{:S(2)}, u32[]{:S(2)}) collective-permute-start(bf16[256,768]{1,0:T(8,128)(2,1)S(1)} %shard_map.110), channel_id=1, source_target_pairs={{0,2},{2,4},{4,6},{6,7},{7,5},{5,3},{3,1},{1,0},{8,10},{10,12},{12... | collective-permute-start | bytes 1179656 | tf_op jit(solution)/shard_map/ppermute | solution.py:608
  140.7 9.6 %collective-permute-start.23 = (bf16[256,768]{1,0:T(8,128)(2,1)S(1)}, bf16[256,768]{1,0:T(8,128)(2,1)S(1)}, u32[]{:S(2)}, u32[]{:S(2)}) collective-permute-start(bf16[256,768]{1,0:T(8,128)(2,1)S(1)} %collective-permute-done.21.refs_6_.refs_4_.refs_2_.refs_0_), channel_id=1, source_target_pairs={{0,2},{2,4},{4,6},{6,7},{7,5},{5,3},{3,1},{1,0},{8,10},{10,12},{12... | collective-permute-start | bytes 1179656 | tf_op jit(solution)/shard_map/ppermute | solution.py:608
  159.1 10.4 %collective-permute-start.27 = (bf16[256,768]{1,0:T(8,128)(2,1)S(1)}, bf16[256,768]{1,0:T(8,128)(2,1)S(1)}, u32[]{:S(2)}, u32[]{:S(2)}) collective-permute-start(bf16[256,768]{1,0:T(8,128)(2,1)S(1)} %shard_map.133), channel_id=1, source_target_pairs={{0,2},{2,4},{4,6},{6,7},{7,5},{5,3},{3,1},{1,0},{8,10},{10,12},{12... | collective-permute-start | bytes 1179656 | tf_op jit(solution)/shard_map/ppermute | solution.py:608
  164.2 10.7 %collective-permute-start.29 = (bf16[512,768]{1,0:T(8,128)(2,1)S(1)}, bf16[512,768]{1,0:T(8,128)(2,1)S(1)}, u32[]{:S(2)}, u32[]{:S(2)}) collective-permute-start(bf16[512,768]{1,0:T(8,128)(2,1)S(1)} %shard_map.125.refs_0_), channel_id=1, source_target_pairs={{0,1},{1,0},{2,3},{3,2},{4,5},{5,4},{6,7},{7,6},{8,9},{9,8},{10,11... | collective-permute-start | bytes 2359304 | tf_op jit(solution)/shard_map/ppermute | solution.py:613
  164.6 10.3 %collective-permute-start.30 = (bf16[512,768]{1,0:T(8,128)(2,1)S(1)}, bf16[512,768]{1,0:T(8,128)(2,1)S(1)}, u32[]{:S(2)}, u32[]{:S(2)}) collective-permute-start(bf16[512,768]{1,0:T(8,128)(2,1)S(1)} %shard_map.126.refs_1_.refs_0_), channel_id=1, source_target_pairs={{0,1},{1,0},{2,3},{3,2},{4,5},{5,4},{6,7},{7,6},{8,9},{9,8},{10,11... | collective-permute-start | bytes 2359304 | tf_op jit(solution)/shard_map/ppermute | solution.py:613
  180.9 12.4 %collective-permute-start.33 = (bf16[64,896]{1,0:T(8,128)(2,1)S(1)}, bf16[64,896]{1,0:T(8,128)(2,1)S(1)}, u32[]{:S(2)}, u32[]{:S(2)}) collective-permute-start(bf16[64,896]{1,0:T(8,128)(2,1)S(1)} %get-tuple-element.66), channel_id=1, source_target_pairs={{0,0},{8,1},{16,2},{24,3},{1,4},{9,5},{17,6},{25,7},{2,8},{10,9},{... | collective-permute-start | bytes 344072 | tf_op jit(solution)/shard_map/ppermute | solution.py:627
  181.6 16.7 %collective-permute-start.34 = (bf16[64,896]{1,0:T(8,128)(2,1)S(1)}, bf16[64,896]{1,0:T(8,128)(2,1)S(1)}, u32[]{:S(2)}, u32[]{:S(2)}) collective-permute-start(bf16[64,896]{1,0:T(8,128)(2,1)S(1)} %get-tuple-element.67), channel_id=1, source_target_pairs={{8,0},{0,1},{24,2},{16,3},{9,4},{1,5},{25,6},{17,7},{10,8},{2,9},{... | collective-permute-start | bytes 344072 | tf_op jit(solution)/shard_map/ppermute | solution.py:627
  184.5 15.8 %collective-permute-start.35 = (bf16[64,896]{1,0:T(8,128)(2,1)S(1)}, bf16[64,896]{1,0:T(8,128)(2,1)S(1)}, u32[]{:S(2)}, u32[]{:S(2)}) collective-permute-start(bf16[64,896]{1,0:T(8,128)(2,1)S(1)} %get-tuple-element.68), channel_id=1, source_target_pairs={{16,0},{24,1},{0,2},{8,3},{17,4},{25,5},{1,6},{9,7},{18,8},{26,9},... | collective-permute-start | bytes 344072 | tf_op jit(solution)/shard_map/ppermute | solution.py:627
  187.1 22.2 %collective-permute-start.36 = (bf16[64,896]{1,0:T(8,128)(2,1)S(1)}, bf16[64,896]{1,0:T(8,128)(2,1)S(1)}, u32[]{:S(2)}, u32[]{:S(2)}) collective-permute-start(bf16[64,896]{1,0:T(8,128)(2,1)S(1)} %get-tuple-element.69), channel_id=1, source_target_pairs={{24,0},{16,1},{8,2},{0,3},{25,4},{17,5},{9,6},{1,7},{26,8},{18,9},... | collective-permute-start | bytes 344072 | tf_op jit(solution)/shard_map/ppermute | solution.py:627
  191.9 17.5 %collective-permute-start.37 = (bf16[64,896]{1,0:T(8,128)(2,1)S(1)}, bf16[64,896]{1,0:T(8,128)(2,1)S(1)}, u32[]{:S(2)}, u32[]{:S(2)}) collective-permute-start(bf16[64,896]{1,0:T(8,128)(2,1)S(1)} %get-tuple-element.70), channel_id=1, source_target_pairs={{1,0},{9,1},{17,2},{25,3},{0,4},{8,5},{16,6},{24,7},{3,8},{11,9},{... | collective-permute-start | bytes 344072 | tf_op jit(solution)/shard_map/ppermute | solution.py:627
  193.3 16.1 %collective-permute-start.38 = (bf16[64,896]{1,0:T(8,128)(2,1)S(1)}, bf16[64,896]{1,0:T(8,128)(2,1)S(1)}, u32[]{:S(2)}, u32[]{:S(2)}) collective-permute-start(bf16[64,896]{1,0:T(8,128)(2,1)S(1)} %get-tuple-element.71), channel_id=1, source_target_pairs={{9,0},{1,1},{25,2},{17,3},{8,4},{0,5},{24,6},{16,7},{11,8},{3,9},{... | collective-permute-start | bytes 344072 | tf_op jit(solution)/shard_map/ppermute | solution.py:627
  198.3 11.1 %collective-permute-start.39 = (bf16[64,896]{1,0:T(8,128)(2,1)S(1)}, bf16[64,896]{1,0:T(8,128)(2,1)S(1)}, u32[]{:S(2)}, u32[]{:S(2)}) collective-permute-start(bf16[64,896]{1,0:T(8,128)(2,1)S(1)} %get-tuple-element.72), channel_id=1, source_target_pairs={{17,0},{25,1},{1,2},{9,3},{16,4},{24,5},{0,6},{8,7},{19,8},{27,9},... | collective-permute-start | bytes 344072 | tf_op jit(solution)/shard_map/ppermute | solution.py:627
  200.3 9.1 %collective-permute-start.40 = (bf16[64,896]{1,0:T(8,128)(2,1)S(1)}, bf16[64,896]{1,0:T(8,128)(2,1)S(1)}, u32[]{:S(2)}, u32[]{:S(2)}) collective-permute-start(bf16[64,896]{1,0:T(8,128)(2,1)S(1)} %get-tuple-element.73), channel_id=1, source_target_pairs={{25,0},{17,1},{9,2},{1,3},{24,4},{16,5},{8,6},{0,7},{27,8},{19,9},... | collective-permute-start | bytes 344072 | tf_op jit(solution)/shard_map/ppermute | solution.py:627
  (29 other events, 185.6 us)
